TPU v7x, 128 devices: a whole 4x4x4 slice. The times are simulated.
128 devices in a mesh: dp: 32 (over y, x_lo, z), row: 2 (over x_hi), col: 2 (over core).
Axes of the slice: x: 4 (x_hi: 2, x_lo: 2; x = x_hi * 2 + x_lo), y: 4, z: 4, core: 2. Of those that a mesh axis runs over, the one named last changes fastest.
Arguments:
- tokens: bfloat16 [8192, 1024], P('dp', ('row', 'col')), may hold values from -6 to 6
- segment_ids: int32 [8192], P('dp'), may hold values from 0 to 31, as said below
- gain_one: float32 [1024], P(('row', 'col')), may hold values from 0.5 to 1.5
- in_weight: bfloat16 [1024, 3, 1024], P('row', None, 'col'), may hold values from -0.1875 to 0.1875
- conv_weight: bfloat16 [1024, 3], P(('col', 'row')), may hold values from -2.5 to 2.5
- out_weight: bfloat16 [1024, 1024], P('col', 'row'), may hold values from -0.1875 to 0.1875
- gain_two: float32 [1024], P(('row', 'col')), may hold values from 0.5 to 1.5
- gate_up: bfloat16 [1024, 2, 4608], P('row', None, 'col'), may hold values from -0.1875 to 0.1875
- down_weight: bfloat16 [4608, 1024], P('col', 'row'), may hold values from -0.125 to 0.125
- cotangent: bfloat16 [8192, 1024], P('dp', ('row', 'col')), may hold values from -6 to 6
Outputs:
- mixed: bfloat16 [8192, 1024], P('dp', ('row', 'col'))
- grad_tokens: bfloat16 [8192, 1024], P('dp', ('row', 'col'))
- grad_gain_one: float32 [1024], P(('row', 'col', 'dp'))
- grad_in: float32 [1024, 3, 1024], P(('row', 'dp'), None, 'col')
- grad_conv: float32 [1024, 3], P(('col', 'row', 'dp'))
- grad_out: float32 [1024, 1024], P(('col', 'dp'), 'row')
- grad_gain_two: float32 [1024], P(('row', 'col', 'dp'))
- grad_gate_up: float32 [1024, 2, 4608], P(('row', 'dp'), None, 'col')
- grad_down: float32 [4608, 1024], P(('col', 'dp'), 'row')
Inputs may be any that keep to these rules, and one draw needn't show every extreme that they name: `segment_ids`: never falling, starting at 0, rising by 0 or 1 from one token to the next; it never rises at a position p with p % 256 below 2 or equal to 255.
All inputs are finite; a program needn't handle non-finite values.
Results may differ from a plain program's by a relative error of at most 0.035.
Values may be sent and summed in bfloat16 or wider, within the bound.
No kernel may reach another device: no remote copies, remote signals or barrier semaphores. Data moves between devices by JAX's collectives and lax.ppermute only.
A program may use at most 128 MiB of HBM per device.

v0:
```python
import functools

import jax
import jax.numpy as jnp
from jax import lax
from jax.experimental import pallas as pl
from jax.experimental.pallas import tpu as pltpu
from jax.sharding import Mesh, PartitionSpec as P

eps_norm = 1e-05
f32 = jnp.float32
low = jnp.bfloat16
SIZES = {"y": 4, "xl": 2, "z": 4, "row": 2, "col": 2}
AXES = tuple(SIZES)


def moved(value, axes, place):
    sizes = [SIZES[a] for a in axes]
    pairs = []
    count = 1
    for size in sizes:
        count *= size
    for source in range(count):
        rest, coords = source, []
        for size in reversed(sizes):
            coords.insert(0, rest % size)
            rest //= size
        target = place(*coords)
        if target is None:
            continue
        index = 0
        for size, at in zip(sizes, target):
            index = index * size + at
        pairs.append((source, index))
    return lax.ppermute(value, axes if len(axes) > 1 else axes[0], pairs)


def ring(value, k):
    return moved(value, ("xl", "row"), lambda xl, row: (xl ^ (k & 1), row ^ (k >> 1)))


def swap_core(value):
    return moved(value, ("col",), lambda col: (1 - col,))


def dot(a, b, dims):
    return lax.dot_general(a, b, (dims, ((), ())), preferred_element_type=f32)


def mm(a, b):
    return dot(a, b, ((1,), (0,)))


def mm_t(a, b):
    return dot(a, b, ((1,), (1,)))


def lanes(index, size):
    return pl.ds(pl.multiple_of(index * size, size), size)


def rows(index, size):
    return pl.ds(pl.multiple_of(index * size, size), size)


def shaped(*shape, kind=f32):
    return jax.ShapeDtypeStruct(shape, kind)


def call(body, outs, scratch, place, *args):
    spec = pl.BlockSpec(memory_space=pltpu.VMEM)
    return pl.pallas_call(
        body,
        out_shape=outs,
        in_specs=[pl.BlockSpec(memory_space=pltpu.SMEM)] + [spec] * len(args),
        out_specs=[spec] * len(outs),
        scratch_shapes=scratch,
        compiler_params=pltpu.CompilerParams(vmem_limit_bytes=56 * 2**20),
    )(place, *args)


def turn(row):
    return jnp.broadcast_to(row, (128, 256)).T


def assemble(out, row, col, near, far):
    for k in range(4):
        at = (row ^ (k >> 1)) * 2
        here = slice((k & 1) * 256, (k & 1) * 256 + 256)
        out[here, lanes(at + col, 256)] = near[k][:256]
        out[here, lanes(at + 1 - col, 256)] = far[k][:256]


def norm_scale(value):
    return lax.rsqrt(jnp.sum(value * value, axis=1, keepdims=True) / 1024 + eps_norm)


def front(place, *refs):
    near, far, w_own = refs[0:4], refs[4:8], refs[8]
    x, n, gain, b, c, u, bx, tails, tail, same_one, same_two, w_far = refs[9:]
    row, xl, col = place[0], place[1], place[2]
    assemble(x, row, col, near, far)
    for k in (0, 2):
        for piece, at in ((near[k], col), (far[k], 1 - col)):
            extra = piece[256:272].astype(f32)
            for i in (0, 1):
                total = extra[3 * i : 3 * i + 1] + extra[3 * i + 1 : 3 * i + 2] + extra[3 * i + 2 : 3 * i + 3]
                gain[8 * i : 8 * i + 8, lanes((row ^ (k >> 1)) * 2 + at, 256)] = jnp.broadcast_to(total, (8, 256))
    for i in (0, 1):
        ids = turn(near[i][256:272].astype(f32)[6:7])
        one = jnp.concatenate([ids[:1], ids[:-1]])
        two = jnp.concatenate([ids[:1], ids[:1], ids[:-2]])
        same_one[256 * i : 256 * i + 256] = jnp.where(ids == one, 1.0, 0.0)
        same_two[256 * i : 256 * i + 256] = jnp.where(ids == two, 1.0, 0.0)

    @pl.loop(0, 8)
    def _(i):
        v = x[rows(i, 64)].astype(f32)
        n[rows(i, 64)] = (v * norm_scale(v) * gain[0:1]).astype(low)

    for i in range(3):
        for e in (0, 1):
            w_far[i, 256 * e : 256 * e + 256] = near[3][272 + 256 * i : 528 + 256 * i, 128 * e : 128 * e + 128]
    n_own, n_far = n[:, lanes(row, 512)], n[:, lanes(1 - row, 512)]
    for i, out in enumerate((b, c, u)):
        out[...] = mm(n_own, w_own[i]) + mm(n_far, w_far[i])
    bx[...] = (b[...] * u[...]).astype(low)
    ends = bx[240:256].astype(f32)[8:], bx[496:512].astype(f32)[8:]
    first = xl == 0
    tails[0] = jnp.where(first, ends[0], ends[1])
    tails[1] = jnp.where(first, ends[1], ends[0])
    tail[...] = jnp.where(first, ends[1], ends[0])


def conv_forward(place, bx, prior, first, c, same_one, same_two, taps, conv, y, y_swap, past_one, past_two):
    xl, zz = place[1], place[4]
    start = zz == 0
    rim = jnp.where(start, first[...], prior[0]), jnp.where(start, prior[0], prior[1])
    for i in (0, 1):
        here = slice(256 * i, 256 * i + 256)
        there = slice(256 - 256 * i, 512 - 256 * i)
        v = bx[here].astype(f32)
        ext = jnp.concatenate([jnp.where(xl == i, rim[0], rim[1]), v])
        one = ext[7:263] * same_one[here]
        two = ext[6:262] * same_two[here]
        past_one[here] = one
        past_two[here] = two
        total = taps[2:3] * v + taps[1:2] * one + taps[0:1] * two
        conv[here] = total
        mixed = (c[here] * total).astype(low)
        y[here] = mixed
        y_swap[there] = mixed


def feed(place, *refs):
    near, far = refs[0:4], refs[4:8]
    x, gain, out_own, out_swap, gu_own, down_own = refs[8:14]
    df_near, df_far, packs = refs[14:18], refs[18:22], refs[22]
    hidden, n, act, dgate, dup, keep, send, df, down_far, out_row = refs[23:33]
    y, wide, gate, up, dact, gu_far, out_far = refs[33:]
    row, xl, col = place[0], place[1], place[2]
    q = 2 * row + xl
    for m in range(16):
        for k in (0, 1):
            for t in range(5):
                at = (5 * k + t) * 32
                gu_far[k, 32 * m : 32 * m + 32, 128 * t : 128 * t + 128] = packs[m, at : at + 32]
        for t in range(4):
            first = 16 * (5 * m // 2)
            at = 320 + 48 * t
            down_far[first : first + 48, 128 * t : 128 * t + 128] = packs[m, at : at + 48]
            for e in (0, 1):
                at = 512 + (4 * e + t) * 32
                out_far[512 * e + 32 * m : 512 * e + 32 * m + 32, 128 * t : 128 * t + 128] = packs[m, at : at + 32]
    out_row[...] = out_far[rows(q, 128)]
    for k in range(4):
        y[:, lanes(col * 4 + (q ^ k), 128)] = near[k][...]
        y[:, lanes((1 - col) * 4 + (q ^ k), 128)] = far[k][...]
    assemble(df, row, col, df_near, df_far)
    y_own, y_far = y[:, lanes(col, 512)], y[:, lanes(1 - col, 512)]
    wide[:, lanes(row, 512)] = mm(y_own, out_own[...]) + mm(y_far, out_swap[...])
    wide[:, lanes(1 - row, 512)] = mm(y_own, out_far[:512]) + mm(y_far, out_far[512:])

    @pl.loop(0, 8)
    def _(i):
        h = x[rows(i, 64)].astype(f32) + wide[rows(i, 64)]
        hidden[rows(i, 64)] = h
        n[rows(i, 64)] = (h * norm_scale(h) * gain[8:9]).astype(low)

    n_own, n_far = n[:, lanes(row, 512)], n[:, lanes(1 - row, 512)]
    gate[...] = mm(n_own, gu_own[0]) + mm(n_far, gu_far[0])
    up[...] = mm(n_own, gu_own[1]) + mm(n_far, gu_far[1])
    dact[...] = mm_t(df[:, lanes(row, 512)], down_own[...]) + mm_t(df[:, lanes(1 - row, 512)], down_far[...])
    lane = lax.broadcasted_iota(jnp.int32, (64, 640), 1) - 64 * xl
    mine = (lane >= 0) & (lane < 576)

    @pl.loop(0, 8)
    def _(i):
        at = rows(i, 64)
        g = jnp.where(mine, gate[at], 0.0)
        v = jnp.where(mine, up[at], 0.0)
        da = dact[at]
        s = 1.0 / (1.0 + jnp.exp(-g))
        gs = g * s
        act[at] = (gs * v).astype(low)
        dgate[at] = (da * v * s * (1.0 + g * (1.0 - s))).astype(low)
        dup[at] = (da * gs).astype(low)

    for k, w in ((0, gu_own), (1, gu_far)):
        wide[:, 512 * k : 512 * k + 512] = mm_t(dgate[...], w[0]) + mm_t(dup[...], w[1])
    part(wide, keep, send, col)


def part(wide, keep, send, col):
    for k in range(4):
        here = slice(256 * (k & 1), 256 * (k & 1) + 256)
        keep[k] = wide[here, lanes(2 * (k >> 1) + col, 256)]
        send[k, :256] = wide[here, lanes(2 * (k >> 1) + 1 - col, 256)].astype(low)


def feed_weights(place, n, act, dgate, dup, df, down_own, down_far, early, keep, send, wide):
    row, xl, col = place[0], place[1], place[2]
    for k, w in ((0, down_own), (1, down_far)):
        wide[:512, 512 * k : 512 * k + 512] = mm(act[...], w[...])
    part(wide, keep, send, col)
    n_t = n[...].T
    for k, g in ((0, dgate), (1, dup)):
        for r in (0, 1):
            total = mm(n_t[512 * r : 512 * r + 512], g[...]).astype(low)
            for m in range(16):
                for t in range(5):
                    at = ((r * 2 + k) * 5 + t) * 32
                    early[m, at : at + 32] = total[32 * m : 32 * m + 32, 128 * t : 128 * t + 128]
    wide[...] = mm(act[...].T, df[...])
    for i in range(8):
        some = wide[pl.ds(pl.multiple_of(64 * xl + 72 * i, 8), 72)]
        some = jnp.concatenate([some, jnp.zeros((8, 1024), f32)]).astype(low)
        for r in (0, 1):
            for t in range(4):
                early[8 * r + i, 640 + 80 * t : 720 + 80 * t] = some[:, 512 * r + 128 * t : 512 * r + 128 * t + 128]


def fold(place, keep, got, own, *others):
    own[...] = keep[0] + got[0].astype(f32)
    for k in (1, 2, 3):
        others[k - 1][...] = (keep[k] + got[k].astype(f32)).astype(low)


def mix_backward(place, *refs):
    near, far = refs[0:4], refs[4:8]
    hidden, df, gain, w_own, w_far, c, conv, same_one, same_two = refs[8:17]
    dh_own, do, dconv, dc, heads, head, dg_two = refs[17:24]
    (dn,) = refs[24:]
    row, xl, col = place[0], place[1], place[2]
    assemble(dn, row, col, near, far)
    own = lanes(2 * row + col, 256)
    dg_two[...] = jnp.zeros((8, 256), f32)

    @pl.loop(0, 8)
    def _(i):
        at = rows(i, 64)
        h = hidden[at]
        r = norm_scale(h)
        d = dn[at].astype(f32)
        scaled = d * gain[8:9]
        total = jnp.sum(scaled * h, axis=1, keepdims=True)
        dh = df[at].astype(f32) + r * scaled - h * (r * r * r * total / 1024)
        do[at] = dh.astype(low)

        @pl.when(i < 4)
        def _():
            h = hidden[at, own]
            d = dn[at, own].astype(f32)
            dh_own[at] = df[at, own].astype(f32) + r * d * gain[8:9, own] - h * (r * r * r * total / 1024)
            dg_two[...] += jnp.broadcast_to(jnp.sum(d * h * r, axis=0, keepdims=True), (8, 256))

    dy = mm_t(do[:, lanes(row, 512)], w_own[...]) + mm_t(do[:, lanes(1 - row, 512)], w_far[...])
    edge = dy * c[...]
    dconv[...] = edge
    dc[...] = dy * conv[...]
    ends = [
        jnp.concatenate([edge[at : at + 8] * same_one[at : at + 8], edge[at : at + 8] * same_two[at : at + 8]])
        for at in (0, 256)
    ]
    first = xl == 0
    heads[0] = jnp.where(first, ends[0], ends[1])
    heads[1] = jnp.where(first, ends[1], ends[0])
    head[...] = jnp.where(first, ends[0], ends[1])


def conv_backward(place, *refs):
    dconv, dc, later, last, same_one, same_two, taps, b, c, u, past_one, past_two, bx, w_own, w_far = refs[:15]
    dproj, keep, send, total, grad_conv = refs[15:20]
    (wide,) = refs[20:]
    xl, col, zz = place[1], place[2], place[4]
    end = zz == 3
    rim = jnp.where(end, later[1], later[0]), jnp.where(end, last[...], later[1])
    parts = []
    for i in (0, 1):
        here = slice(256 * i, 256 * i + 256)
        d = dconv[here]
        edge = jnp.where(xl == i, rim[0], rim[1])
        one = jnp.concatenate([d * same_one[here], edge[:8]])
        two = jnp.concatenate([d * same_two[here], edge[8:]])
        dbx = taps[2:3] * d + taps[1:2] * one[1:257] + taps[0:1] * two[2:258]
        parts.append(jnp.concatenate([
            jnp.sum(d * past_two[here], axis=0, keepdims=True),
            jnp.sum(d * past_one[here], axis=0, keepdims=True),
            jnp.sum(d * bx[here].astype(f32), axis=0, keepdims=True),
            jnp.zeros((5, 128), f32),
        ]))
        db = (dbx * u[here]).astype(low)
        dcv = dc[here].astype(low)
        du = (dbx * b[here]).astype(low)
        dproj[here, 0:128] = db
        dproj[here, 128:256] = dcv
        dproj[here, 256:384] = du
        mass = jnp.sum(
            db.astype(f32) * b[here] + dcv.astype(f32) * c[here] + du.astype(f32) * u[here], axis=1, keepdims=True
        )
        line = jnp.broadcast_to(mass, (256, 128)).T[:8]
        total[i] = line
        high = line.astype(low)
        rest = (line - high.astype(f32)).astype(low)
        both = jnp.concatenate([high, rest])
        send[i, 256:272] = both
        send[2 + i, 256:272] = both
    grad_conv[...] = parts[0] + parts[1]
    for k, w in ((0, w_own), (1, w_far)):
        whole = jnp.concatenate([w[0], w[1], w[2]], axis=1)
        wide[:, 512 * k : 512 * k + 512] = mm_t(dproj[...], whole)
    part(wide, keep, send, col)


def mix_weights(place, n, dproj, y, do, small, late):
    n_t = n[...].T
    for r in (0, 1):
        total = mm(n_t[512 * r : 512 * r + 512], dproj[...]).astype(low)
        for m in range(16):
            for h in (0, 1):
                for k in range(3):
                    late[m, 2 * r + h, 16 * k : 16 * k + 16] = total[
                        32 * m + 16 * h : 32 * m + 16 * h + 16, 128 * k : 128 * k + 128
                    ]
                late[m, 2 * r + h, 48:64] = small[r]
    total = mm(y[...].T, do[...]).astype(low)
    for r in (0, 1):
        for i in range(8):
            for t in range(4):
                late[8 * r + i, 4, 16 * t : 16 * t + 16] = total[
                    16 * i : 16 * i + 16, 512 * r + 128 * t : 512 * r + 128 * t + 128
                ]


def fold_last(place, keep, got, keep_ffn, got_ffn, total, x, dg_two, grad_conv, own, own_ffn, mass, *rest):
    others, small = rest[:3], rest[3]
    row, xl, col = place[0], place[1], place[2]
    sums = [jnp.zeros((1, 256), f32), jnp.zeros((1, 256), f32)]
    scale = norm_scale(x[...].astype(f32))
    for k in range(4):
        whole = keep[k] + got[k, :256].astype(f32)
        line = total[k & 1] + got[k, 256:264].astype(f32) + got[k, 264:272].astype(f32)
        ffn = keep_ffn[k] + got_ffn[k].astype(f32)
        if k == 0:
            own[...] = whole
            own_ffn[...] = ffn
            mass[...] = line
        else:
            others[k - 1][272:528] = ffn.astype(low)
            others[k - 1][:256] = whole.astype(low)
            high = line.astype(low)
            others[k - 1][256:272] = jnp.concatenate([high, (line - high.astype(f32)).astype(low)])
        at = (k & 1) * 256
        v = x[at : at + 256, lanes((row ^ (k >> 1)) * 2 + col, 256)].astype(f32)
        sums[k >> 1] += jnp.sum(whole * v * scale[at : at + 256], axis=0, keepdims=True)
    zero = jnp.zeros((1, 128), f32)
    pair = lambda v: [v[:, :128], v[:, 128:]]
    taps = []
    for a in range(3):
        w = grad_conv[a : a + 1]
        taps += [jnp.where(xl == 0, w, zero), jnp.where(xl == 0, zero, w)]
    small[row] = jnp.concatenate(pair(sums[0]) + pair(dg_two[0:1]) + taps + [zero] * 6).astype(low)
    small[1 - row] = jnp.concatenate(pair(sums[1]) + [zero] * 14).astype(low)


def finish(place, own, own_ffn, mass, got1, got2, got3, dh, hidden, x, gain, out, mixed):
    row, col = place[0], place[2]
    here = lanes(2 * row + col, 256)
    total, line, ffn = own[...], mass[...], own_ffn[...]
    for got in (got1, got2, got3):
        total += got[:256].astype(f32)
        ffn += got[272:528].astype(f32)
        line += got[256:264].astype(f32) + got[264:272].astype(f32)
    scale = norm_scale(x[:256].astype(f32))
    column = turn(line[0:1])
    column = jnp.concatenate([column, column], axis=1)
    v = x[:256, here].astype(f32)
    mixed[...] = (hidden[...] + ffn).astype(low)
    out[...] = (dh[...] + scale * gain[0:1, here] * total - v * (scale * scale) * column / 1024).astype(low)


def local(
    tokens,
    segment_ids,
    gain_one,
    in_weight,
    conv_weight,
    out_weight,
    gain_two,
    gate_up,
    down_weight,
    cotangent,
):
    yy, xl, zz, row, col = (lax.axis_index(a) for a in AXES)
    q = 2 * row + xl
    place = jnp.stack([row, xl, col, yy, zz]).astype(jnp.int32)

    def cut(value, index, size, axis):
        return lax.dynamic_slice_in_dim(value, index * size, size, axis)

    def window(value, index, axis):
        return lax.dynamic_slice_in_dim(value, (9 * index // 2) * 128, 640, axis)

    extra = []
    for gain in (gain_one, gain_two):
        for _ in range(3):
            piece = lax.reduce_precision(gain, 8, 7)
            extra.append(piece)
            gain = gain - piece
    extra.append(segment_ids.astype(f32))
    extra = jnp.pad(jnp.stack(extra), ((0, 9), (0, 0))).astype(low)
    piece = jnp.concatenate([tokens, extra])
    in_w = in_weight.transpose(1, 0, 2)
    in_own, in_send = cut(in_w, q, 128, 2), cut(in_w, 3 - q, 128, 2)
    in_send = jnp.concatenate([in_send[:, :256], in_send[:, 256:]], axis=2).reshape(768, 256)
    near = [piece, ring(piece, 1), ring(piece, 2), ring(jnp.concatenate([piece, in_send]), 3)]
    far = [swap_core(v) for v in near[:3]] + [swap_core(near[3][:272])]
    taps = jnp.pad(cut(conv_weight, xl, 128, 0).T.astype(f32), ((0, 5), (0, 0)))

    def begin(index):
        return (9 * index // 2) * 128

    m = 4 * yy + zz
    gu_part = lax.dynamic_slice(gate_up, (32 * m, 0, begin(3 - q)), (32, 2, 640))
    gu_part = gu_part.reshape(32, 2, 5, 128).transpose(1, 2, 0, 3).reshape(320, 128)
    down_part = lax.dynamic_slice(down_weight, (begin(3 - q) + 16 * (5 * m // 2), 0), (48, 512))
    down_part = down_part.reshape(48, 4, 128).transpose(1, 0, 2).reshape(192, 128)
    out_part = cut(out_weight, m, 32, 0).reshape(32, 4, 128).transpose(1, 0, 2).reshape(128, 128)
    pack = ring(jnp.concatenate([gu_part, down_part, out_part]), 3)
    cross = moved(out_part, ("xl", "row", "col"), lambda xl, row, col: (1 - xl, 1 - row, 1 - col))
    packs = lax.all_gather(jnp.concatenate([pack, cross]), ("y", "z"))
    out_swap = swap_core(out_weight)
    gu_own, down_own = window(gate_up.transpose(1, 0, 2), q, 2), window(down_weight, q, 0)

    tile = shaped(512, 128)
    tile_low = shaped(512, 128, kind=low)
    whole_low = shaped(512, 1024, kind=low)
    x, n_one, gain, b, c, u, bx, tails, tail, same_one, same_two = call(
        front,
        [whole_low, whole_low, shaped(16, 1024), tile, tile, tile, tile_low, shaped(2, 8, 128), shaped(8, 128), tile, tile],
        [pltpu.VMEM((3, 512, 128), low)],
        place,
        *near,
        *far,
        in_own,
    )
    in_far = near[3][272:].reshape(3, 256, 2, 128).transpose(0, 2, 1, 3).reshape(3, 512, 128)
    df, tails = lax.optimization_barrier((cotangent, tails))
    df_near = [df] + [ring(df, k) for k in (1, 2, 3)]
    df_far = [swap_core(v) for v in df_near]
    prior = moved(tails, ("z",), lambda z: ((z + 1) % 4,))
    first = moved(tail, ("y", "z"), lambda y, z: (y + 1, 0) if z == 3 and y < 3 else None)
    conv, y, y_swap, past_one, past_two = call(
        conv_forward, [tile, tile_low, tile_low, tile, tile], [], place, bx, prior, first, c, same_one, same_two, taps
    )
    near = [y, ring(y_swap, 1), ring(y, 2), ring(y_swap, 3)]
    far = [swap_core(v) for v in near]

    hid_low = shaped(512, 640, kind=low)
    keep4, send4 = shaped(4, 256, 256), shaped(4, 256, 256, kind=low)
    send4_mass = shaped(4, 272, 256, kind=low)
    hidden, n_two, act, dgate, dup, keep, send, df, down_far, out_row = call(
        feed,
        [
            shaped(512, 1024),
            whole_low,
            hid_low,
            hid_low,
            hid_low,
            keep4,
            send4,
            whole_low,
            shaped(640, 512, kind=low),
            shaped(128, 512, kind=low),
        ],
        [
            pltpu.VMEM((512, 1024), low),
            pltpu.VMEM((512, 1024), f32),
            pltpu.VMEM((512, 640), f32),
            pltpu.VMEM((512, 640), f32),
            pltpu.VMEM((512, 640), f32),
            pltpu.VMEM((2, 512, 640), low),
            pltpu.VMEM((1024, 512), low),
        ],
        place,
        *near,
        *far,
        x,
        gain,
        out_weight,
        out_swap,
        gu_own,
        down_own,
        *df_near,
        *df_far,
        packs,
    )
    got = swap_core(send)
    own = shaped(256, 256)
    own_low = shaped(256, 256, kind=low)
    dn_own, *parts = call(fold, [own, own_low, own_low, own_low], [], place, keep, got)
    ringed = [ring(v, k) for k, v in zip((1, 2, 3), parts)]
    n_two, dn_own, *parts = lax.optimization_barrier((n_two, dn_own, *parts))
    early, keep_ffn, send_ffn = call(
        feed_weights,
        [shaped(16, 960, 128, kind=low), keep4, send4],
        [pltpu.VMEM((640, 1024), f32)],
        place,
        n_two,
        act,
        dgate,
        dup,
        df,
        down_own,
        down_far,
    )
    dn_own, early = lax.optimization_barrier((dn_own, early))
    early = early.reshape(16 * 960, 128)
    early = lax.psum_scatter(early, ("y", "z"), scatter_dimension=0, tiled=True)
    got_ffn = swap_core(send_ffn)
    piece = (dn_own + sum(v.astype(f32) for v in ringed)).astype(low)
    near = [piece] + [ring(piece, k) for k in (1, 2, 3)]
    far = [swap_core(v) for v in near]
    dh_own, do, dconv, dc, heads, head, dg_two = call(
        mix_backward,
        [own, whole_low, tile, tile, shaped(2, 16, 128), shaped(16, 128), shaped(8, 256)],
        [pltpu.VMEM((512, 1024), low)],
        place,
        *near,
        *far,
        hidden,
        df,
        gain,
        cut(out_weight, q, 128, 0),
        out_row,
        c,
        conv,
        same_one,
        same_two,
    )
    later = moved(heads, ("z",), lambda z: ((z - 1) % 4,))
    last = moved(head, ("y", "z"), lambda y, z: (y - 1, 3) if z == 0 and y > 0 else None)
    dproj, keep, send, total, grad_conv = call(
        conv_backward,
        [shaped(512, 384, kind=low), keep4, send4_mass, shaped(2, 8, 256), shaped(8, 128)],
        [pltpu.VMEM((512, 1024), f32)],
        place,
        dconv,
        dc,
        later,
        last,
        same_one,
        same_two,
        taps,
        b,
        c,
        u,
        past_one,
        past_two,
        bx,
        in_own,
        in_far,
    )
    got = swap_core(send)
    own_mass = shaped(528, 256, kind=low)
    dn_own, ffn_own, mass, *parts, small = call(
        fold_last,
        [own, own, shaped(8, 256), own_mass, own_mass, own_mass, shaped(2, 16, 128, kind=low)],
        [],
        place,
        keep,
        got,
        keep_ffn,
        got_ffn,
        total,
        x,
        dg_two,
        grad_conv,
    )
    (late,) = call(mix_weights, [shaped(16, 5, 64, 128, kind=low)], [], place, n_one, dproj, y, do, small)
    ringed = [ring(v, k) for k, v in zip((1, 2, 3), parts)]
    late = lax.all_to_all(late, ("y", "z"), 0, 0)
    h_own = lax.dynamic_slice_in_dim(hidden[:256], (2 * row + col) * 256, 256, 1)
    grad_tokens, mixed = call(
        finish, [own_low, own_low], [], place, dn_own, ffn_own, mass, *ringed, dh_own, h_own, x, gain
    )

    def settle(value):
        return moved(
            value,
            ("y", "xl", "z", "row"),
            lambda y, xl, z, r: (2 * r + xl, y % 2, z, y // 2),
        ).astype(f32)

    spot = 2 * row + zz % 2

    def spread(pick):
        got = jnp.stack(
            [
                moved(
                    pick(row ^ (j >> 1), xl ^ (j & 1)),
                    ("y", "xl", "z", "row"),
                    lambda y, xl, z, r, j=j: (y, z // 2, 2 * (z % 2) + (xl ^ (j & 1)), r ^ (j >> 1)),
                )
                for j in range(4)
            ]
        )
        return [lax.dynamic_index_in_dim(got, spot ^ k, 0, keepdims=False) for k in range(4)]

    gu_early = early[:640].reshape(2, 10, 2, 16, 128)
    down_early = early[640:].reshape(4, 80, 128)[:, :72].transpose(1, 0, 2).reshape(72, 512)
    gu_got = spread(lambda r, half: lax.dynamic_slice(gu_early, (r, 0, half, 0, 0), (1, 10, 1, 16, 128)).reshape(2, 5, 16, 128))
    gu_got = [w.astype(f32) for w in gu_got]
    grad_gate_up = jnp.concatenate(
        [
            gu_got[0][:, :4],
            gu_got[0][:, 4:] + gu_got[1][:, :1],
            gu_got[1][:, 1:],
            gu_got[2][:, :4],
            gu_got[2][:, 4:] + gu_got[3][:, :1],
            gu_got[3][:, 1:],
        ],
        axis=1,
    )
    grad_gate_up = grad_gate_up.transpose(2, 0, 1, 3).reshape(16, 2, 2304)
    grad_down = settle(down_early)

    late = jnp.sum(late.astype(f32), axis=0).astype(low)
    grad_out = settle(late[4].reshape(4, 16, 128).transpose(1, 0, 2).reshape(16, 512))
    in_got = spread(lambda r, half: lax.dynamic_index_in_dim(late, 2 * r + half, 0, keepdims=False))
    grad_in = jnp.concatenate(
        [w[:48].reshape(3, 16, 128).transpose(1, 0, 2) for w in in_got], axis=-1
    ).astype(f32)
    small = sum(w[48:].astype(f32) for w in in_got)[:10].reshape(5, 256)
    small = cut(small, 8 * yy + 4 * xl + zz, 8, 1)
    return (
        mixed,
        grad_tokens,
        small[0],
        grad_in,
        small[2:5].T,
        grad_out,
        small[1],
        grad_gate_up,
        grad_down,
    )


def solution(mesh):
    dp = ("y", "xl", "z")
    fine = Mesh(mesh.devices.reshape(tuple(SIZES.values())), AXES)
    return jax.shard_map(
        local,
        mesh=fine,
        in_specs=(
            P(dp, ("row", "col")),
            P(dp),
            P(("row", "col")),
            P("row", None, "col"),
            P(("col", "row"), None),
            P("col", "row"),
            P(("row", "col")),
            P("row", None, "col"),
            P("col", "row"),
            P(dp, ("row", "col")),
        ),
        out_specs=(
            P(dp, ("row", "col")),
            P(dp, ("row", "col")),
            P(("row", "col", *dp)),
            P(("row", *dp), None, "col"),
            P(("col", "row", *dp), None),
            P(("col", *dp), "row"),
            P(("row", "col", *dp)),
            P(("row", *dp), None, "col"),
            P(("col", *dp), "row"),
        ),
        check_vma=False,
    )
```

profile of v0, /device:TPU:38, one launch (start us, length us, event | category | flops | bytes accessed | tf_op | source)
XLA Modules:
  0.0 242.1 jit_solution(8669198573466870466)
XLA Ops:
  12.5 4.3 %collective-permute-done.25 = bf16[128,128]{1,0:T(8,128)(2,1)S(1)} collective-permute-done((bf16[128,128]{1,0:T(8,128)(2,1)S(1)}, bf16[128,128]{1,0:T(8,128)(2,1)S(1)}, u32[]{:S(2)}, u32[]{:S(2)}) %collective-permute-start.25) | collective-permute-done | bytes 32800 | tf_op jit(solution)/shard_map/ppermute | solution.py:35
  25.0 5.0 %collective-permute-done.1.refs_2_ = bf16[272,256]{1,0:T(8,128)(2,1)} collective-permute-done((bf16[272,256]{1,0:T(8,128)(2,1)S(1)}, bf16[272,256]{1,0:T(8,128)(2,1)}, u32[]{:S(2)}, u32[]{:S(2)}) %collective-permute-start.1) | collective-permute-done | bytes 139296 | tf_op jit(solution)/shard_map/ppermute | solution.py:35
  32.2 7.0 %collective-permute-done.2.refs_3_ = bf16[1040,256]{1,0:T(8,128)(2,1)S(1)} collective-permute-done((bf16[1040,256]{1,0:T(8,128)(2,1)S(1)}, bf16[1040,256]{1,0:T(8,128)(2,1)S(1)}, u32[]{:S(2)}, u32[]{:S(2)}) %collective-permute-start.2) | collective-permute-done | bytes 532512 | tf_op jit(solution)/shard_map/ppermute | solution.py:35
  41.6 4.6 %shard_map.169 = (bf16[512,1024]{1,0:T(8,128)(2,1)}, bf16[512,1024]{1,0:T(8,128)(2,1)}, f32[16,1024]{1,0:T(8,128)}, f32[512,128]{1,0:T(8,128)}, f32[512,128]{1,0...) custom-call(s32[5]{0:T(128)} %stack.85.place, ...), custom_call_target="tpu_custom_call" | custom-call | tf_op jit(solution)/shard_map/pallas_call | solution.py:72
  50.1 3.0 %collective-permute-start.17 = (bf16[256,256]{1,0:T(8,128)(2,1)}, bf16[256,256]{1,0:T(8,128)(2,1)S(1)}, u32[]{:S(2)}, u32[]{:S(2)}) collective-permute-start(bf16[256,256]{1,0:T(8,128)(2,1)} %refs_14_), channel_id=1, source_target_pairs={{0,16},{2,18},{16,0},{18,2},{1,17},{3,19},{17,1},{19,3},{4,20},{6,... | collective-permute-start | bytes 393224 | tf_op jit(solution)/shard_map/ppermute | solution.py:35
  63.8 3.6 %collective-permute-done.10.refs_2_ = bf16[512,128]{1,0:T(8,128)(2,1)S(1)} collective-permute-done((bf16[512,128]{1,0:T(8,128)(2,1)}, bf16[512,128]{1,0:T(8,128)(2,1)S(1)}, u32[]{:S(2)}, u32[]{:S(2)}) %collective-permute-start.10) | collective-permute-done | bytes 131104 | tf_op jit(solution)/shard_map/ppermute | solution.py:35
  73.8 14.2 %shard_map.171 = (f32[512,1024]{1,0:T(8,128)}, bf16[512,1024]{1,0:T(8,128)(2,1)}, bf16[512,640]{1,0:T(8,128)(2,1)}, bf16[512,640]{1,0:T(8,128)(2,1)}, bf16[512,6...) custom-call(s32[5]{0:T(128)} %stack.85.place, ...), custom_call_target="tpu_custom_call" | custom-call | tf_op jit(solution)/shard_map/pallas_call | solution.py:72
  93.4 8.1 %shard_map.173 = (bf16[16,960,128]{2,1,0:T(8,128)(2,1)}, f32[4,256,256]{2,1,0:T(8,128)}, bf16[4,256,256]{2,1,0:T(8,128)(2,1)}) custom-call(s32[5]{0:T(128)} %stack.85.place, bf16[512,1024]{1,0:T(8,128)(2,1)} %get-tuple-element.89.n, bf16[512,640]{1,0:T(8,128)(2,1)} %get-tuple-element.90.act, bf16[512,640]{1,0:T(8,128)(2,1)} %get-tuple-element.91.dgate, ...), custom_call_target="tpu_custom_call" | custom-call | tf_op jit(solution)/shard_map/pallas_call | solution.py:72
  117.6 3.8 %collective-permute-done.32.refs_3_ = bf16[256,256]{1,0:T(8,128)(2,1)S(1)} collective-permute-done((bf16[256,256]{1,0:T(8,128)(2,1)S(1)}, bf16[256,256]{1,0:T(8,128)(2,1)S(1)}, u32[]{:S(2)}, u32[]{:S(2)}) %collective-permute-start.32) | collective-permute-done | bytes 131104 | tf_op jit(solution)/shard_map/ppermute | solution.py:35
  126.6 5.6 %shard_map.174 = (f32[256,256]{1,0:T(8,128)}, bf16[512,1024]{1,0:T(8,128)(2,1)}, f32[512,128]{1,0:T(8,128)}, f32[512,128]{1,0:T(8,128)}, f32[2,16,128]{2,1,0:T(8...) custom-call(s32[5]{0:T(128)} %stack.85.place, bf16[256,256]{1,0:T(8,128)(2,1)} %copy-done.6, bf16[256,256]{1,0:T(8,128)(2,1)} %copy-done.25, ...), custom_call_target="tpu_custom_call" | custom-call | tf_op jit(solution)/shard_map/pallas_call | solution.py:72
  137.1 4.1 %shard_map.175 = (bf16[512,384]{1,0:T(8,128)(2,1)}, f32[4,256,256]{2,1,0:T(8,128)}, bf16[4,272,256]{2,1,0:T(8,128)(2,1)}, f32[2,8,256]{2,1,0:T(8,128)}, f32[8,128]{1,0:T(8,128)}) custom-call(s32[5]{0:T(128)} %stack.85.place, f32[512,128]{1,0:T(8,128)} %get-tuple-element.100.refs_0_, f32[512,128]{1,0:T(8,128)} %get-tuple-element.101.refs_1_, ...), custom_call_target="tpu_custom_call" | custom-call | tf_op jit(solution)/shard_map/pallas_call | solution.py:72
  144.9 3.7 %shard_map.176 = (f32[256,256]{1,0:T(8,128)}, f32[256,256]{1,0:T(8,128)}, f32[8,256]{1,0:T(8,128)}, bf16[528,256]{1,0:T(8,128)(2,1)}, bf16[528,256]{1,0:T(8,128)...) custom-call(s32[5]{0:T(128)} %stack.85.place, f32[4,256,256]{2,1,0:T(8,128)} %get-tuple-element.108.keep, ...), custom_call_target="tpu_custom_call" | custom-call | tf_op jit(solution)/shard_map/pallas_call | solution.py:72
  148.6 3.8 %shard_map.178 = bf16[16,5,64,128]{3,2,1,0:T(8,128)(2,1)} custom-call(s32[5]{0:T(128)} %stack.85.place, bf16[512,1024]{1,0:T(8,128)(2,1)} %get-tuple-element.124.n, bf16[512,384]{1,0:T(8,128)(2,1)} %get-tuple-element.125.dproj, bf16[512,128]{1,0:T(8,128)(2,1)} %get-tuple-element.76.refs_0_.y, bf16[512,1024]{1,0:T(8,128)(2,1)} %get-tuple-element.126.do, ...), custom_call_target="tpu_custom_call" | custom-call | tf_op jit(solution)/shard_map/pallas_call | solution.py:72
  152.4 12.7 %all-to-all-start = ((bf16[16,5,64,128]{3,2,1,0:T(8,128)(2,1)}), bf16[16,5,64,128]{3,2,1,0:T(8,128)(2,1)}, u32[]{:S(2)}, u32[]{:S(2)}) async-start(bf16[16,5,64,128]{3,2,1,0:T(8,128)(2,1)} %shard_map.178), calls=%async_computation | async-start | bytes 2621440 | tf_op jit(solution)/shard_map/all_to_all | solution.py:602
  165.1 2.9 %collective-permute-start.42 = (bf16[528,256]{1,0:T(8,128)(2,1)}, bf16[528,256]{1,0:T(8,128)(2,1)}, u32[]{:S(2)}, u32[]{:S(2)}) collective-permute-start(bf16[528,256]{1,0:T(8,128)(2,1)} %get-tuple-element.119), channel_id=1, source_target_pairs={{0,2},{2,0},{16,18},{18,16},{1,3},{3,1},{17,19},{19,17},{4,6},{6,4... | collective-permute-start | bytes 811016 | tf_op jit(solution)/shard_map/ppermute | solution.py:35
  171.2 16.1 %all-to-all-done = bf16[16,5,64,128]{3,2,1,0:T(8,128)(2,1)} async-done(((bf16[16,5,64,128]{3,2,1,0:T(8,128)(2,1)}), bf16[16,5,64,128]{3,2,1,0:T(8,128)(2,1)}, u32[]{:S(2)}, u32[]{:S(2)}) %all-to-all-start) | async-done | bytes 1310752 | tf_op jit(solution)/shard_map/all_to_all | solution.py:602
  193.1 4.6 %collective-permute-start.44 = (bf16[64,128]{1,0:T(8,128)(2,1)S(1)}, bf16[64,128]{1,0:T(8,128)(2,1)S(1)}, u32[]{:S(2)}, u32[]{:S(2)}) collective-permute-start(bf16[64,128]{1,0:T(8,128)(2,1)S(1)} %get-tuple-element.163), channel_id=1, source_target_pairs={{0,0},{2,2},{4,8},{6,10},{8,16},{10,18},{12,24},{14,26},{16,4},{18... | collective-permute-start | bytes 49160 | tf_op jit(solution)/shard_map/ppermute | solution.py:35
  198.4 2.8 %shard_map.177 = (bf16[256,256]{1,0:T(8,128)(2,1)}, bf16[256,256]{1,0:T(8,128)(2,1)}) custom-call(s32[5]{0:T(128)} %stack.85.place, f32[256,256]{1,0:T(8,128)} %get-tuple-element.115.own, f32[256,256]{1,0:T(8,128)} %get-tuple-element.116.own_ffn, f32[8,256]{1,0:T(8,128)} %get-tuple-element.117.mass, bf16[528,256]{1,0:T(8,128)(2,1)} %collective-permute-done.41.got1, ...), custom_call_target="tpu_custom_call" | custom-call | tf_op jit(solution)/shard_map/pallas_call | solution.py:72
  201.2 3.7 %collective-permute-start.48 = (bf16[16,512]{1,0:T(8,128)(2,1)S(1)}, bf16[16,512]{1,0:T(8,128)(2,1)S(1)}, u32[]{:S(2)}, u32[]{:S(2)}) collective-permute-start(bf16[16,512]{1,0:T(8,128)(2,1)S(1)} %bitcast.122), channel_id=1, source_target_pairs={{0,0},{2,64},{4,4},{6,68},{8,8},{10,72},{12,12},{14,76},{16,32},{1... | collective-permute-start | bytes 49160 | tf_op jit(solution)/shard_map/ppermute | solution.py:35
  205.0 5.3 %collective-permute-done.48 = bf16[16,512]{1,0:T(8,128)(2,1)S(1)} collective-permute-done((bf16[16,512]{1,0:T(8,128)(2,1)S(1)}, bf16[16,512]{1,0:T(8,128)(2,1)S(1)}, u32[]{:S(2)}, u32[]{:S(2)}) %collective-permute-start.48) | collective-permute-done | bytes 16416 | tf_op jit(solution)/shard_map/ppermute | solution.py:35
  213.8 3.8 %collective-permute-start.49 = (bf16[2,5,16,128]{3,2,1,0:T(8,128)(2,1)S(1)}, bf16[2,5,16,128]{3,2,1,0:T(8,128)(2,1)S(1)}, u32[]{:S(2)}, u32[]{:S(2)}) collective-permute-start(bf16[2,5,16,128]{3,2,1,0:T(8,128)(2,1)S(1)} %bitcast.117), channel_id=1, source_target_pairs={{0,0},{2,2},{4,8},{6,10},{8,16},{10,18},{12,24},{14,26},{16,4},{18... | collective-permute-start | bytes 122888 | tf_op jit(solution)/shard_map/ppermute | solution.py:35
  217.6 4.9 %collective-permute-start.51 = (bf16[2,5,16,128]{3,2,1,0:T(8,128)(2,1)S(1)}, bf16[2,5,16,128]{3,2,1,0:T(8,128)(2,1)S(1)}, u32[]{:S(2)}, u32[]{:S(2)}) collective-permute-start(bf16[2,5,16,128]{3,2,1,0:T(8,128)(2,1)S(1)} %bitcast.115), channel_id=1, source_target_pairs={{0,2},{2,0},{4,10},{6,8},{8,18},{10,16},{12,26},{14,24},{16,6},{18... | collective-permute-start | bytes 122888 | tf_op jit(solution)/shard_map/ppermute | solution.py:35
  224.5 3.7 %collective-permute-start.53 = (bf16[72,512]{1,0:T(8,128)(2,1)S(1)}, bf16[72,512]{1,0:T(8,128)(2,1)S(1)}, u32[]{:S(2)}, u32[]{:S(2)}) collective-permute-start(bf16[72,512]{1,0:T(8,128)(2,1)S(1)} %copy_bitcast_fusion.1), channel_id=1, source_target_pairs={{0,0},{2,64},{4,4},{6,68},{8,8},{10,72},{12,12},{14,76},{16,32},{1... | collective-permute-start | bytes 221192 | tf_op jit(solution)/shard_map/ppermute | solution.py:35
  229.3 5.3 %collective-permute-done.53 = bf16[72,512]{1,0:T(8,128)(2,1)S(1)} collective-permute-done((bf16[72,512]{1,0:T(8,128)(2,1)S(1)}, bf16[72,512]{1,0:T(8,128)(2,1)S(1)}, u32[]{:S(2)}, u32[]{:S(2)}) %collective-permute-start.53) | collective-permute-done | bytes 73760 | tf_op jit(solution)/shard_map/ppermute | solution.py:35
  (255 shorter events, 90.4 us)
Async XLA Ops:
  7.2 66.6 %all-gather.3.cloned.1.call-start = ((), (), s32[]{:S(2)}) async-start(), calls=%async_computation.3 | async-start | bytes 3342336 | tf_op jit(solution)/shard_map/all_gather | solution.py:451
  18.4 194.5 %reduce-scatter.2.cloned.1.call-start = ((), (), s32[]{:S(2)}) async-start(), calls=%async_computation.2 | async-start | bytes 4177920 | tf_op jit(solution)/shard_map/reduce_scatter | solution.py:539
  20.7 18.5 %collective-permute-start.2 = (bf16[1040,256]{1,0:T(8,128)(2,1)S(1)}, bf16[1040,256]{1,0:T(8,128)(2,1)S(1)}, u32[]{:S(2)}, u32[]{:S(2)}) collective-permute-start(bf16[1040,256]{1,0:T(8,128)(2,1)S(1)} %pad_maximum_fusion), channel_id=1, source_target_pairs={{0,18},{2,16},{16,2},{18,0},{1,19},{3,17},{17,3},{19,1},{4,22},{6,... | collective-permute-start | bytes 1597448 | tf_op jit(solution)/shard_map/ppermute | solution.py:35
  21.6 35.0 %collective-permute-start.16 = (bf16[512,512]{1,0:T(8,128)(2,1)S(1)}, bf16[512,512]{1,0:T(8,128)(2,1)}, u32[]{:S(2)}, u32[]{:S(2)}) collective-permute-start(bf16[512,512]{1,0:T(8,128)(2,1)S(1)} %copy-done.2), channel_id=1, source_target_pairs={{0,1},{1,0},{2,3},{3,2},{4,5},{5,4},{6,7},{7,6},{8,9},{9,8},{10,11... | collective-permute-start | bytes 1572872 | tf_op jit(solution)/shard_map/ppermute | solution.py:35
  22.6 9.6 %collective-permute-start = (bf16[272,256]{1,0:T(8,128)(2,1)S(1)}, bf16[272,256]{1,0:T(8,128)(2,1)}, u32[]{:S(2)}, u32[]{:S(2)}) collective-permute-start(bf16[272,256]{1,0:T(8,128)(2,1)S(1)} %pad_maximum_fusion.5.refs_0_), channel_id=1, source_target_pairs={{0,16},{2,18},{16,0},{18,2},{1,17},{3,19},{17,1},{19,3},{4,20},{6,... | collective-permute-start | bytes 417800 | tf_op jit(solution)/shard_map/ppermute | solution.py:35
  25.0 15.5 %collective-permute-start.3 = (bf16[272,256]{1,0:T(8,128)(2,1)S(1)}, bf16[272,256]{1,0:T(8,128)(2,1)}, u32[]{:S(2)}, u32[]{:S(2)}) collective-permute-start(bf16[272,256]{1,0:T(8,128)(2,1)S(1)} %pad_maximum_fusion.5.refs_0_), channel_id=1, source_target_pairs={{0,1},{1,0},{2,3},{3,2},{4,5},{5,4},{6,7},{7,6},{8,9},{9,8},{10,11... | collective-permute-start | bytes 417800 | tf_op jit(solution)/shard_map/ppermute | solution.py:35
  30.0 10.5 %collective-permute-start.5 = (bf16[272,256]{1,0:T(8,128)(2,1)}, bf16[272,256]{1,0:T(8,128)(2,1)}, u32[]{:S(2)}, u32[]{:S(2)}) collective-permute-start(bf16[272,256]{1,0:T(8,128)(2,1)} %collective-permute-done.1.refs_2_), channel_id=1, source_target_pairs={{0,1},{1,0},{2,3},{3,2},{4,5},{5,4},{6,7},{7,6},{8,9},{9,8},{10,11... | collective-permute-start | bytes 417800 | tf_op jit(solution)/shard_map/ppermute | solution.py:35
  48.9 10.1 %collective-permute-start.19 = (bf16[256,256]{1,0:T(8,128)(2,1)}, bf16[256,256]{1,0:T(8,128)(2,1)S(1)}, u32[]{:S(2)}, u32[]{:S(2)}) collective-permute-start(bf16[256,256]{1,0:T(8,128)(2,1)} %refs_14_), channel_id=1, source_target_pairs={{0,18},{2,16},{16,2},{18,0},{1,19},{3,17},{17,3},{19,1},{4,22},{6,... | collective-permute-start | bytes 393224 | tf_op jit(solution)/shard_map/ppermute | solution.py:35
  49.7 9.4 %collective-permute-start.18 = (bf16[256,256]{1,0:T(8,128)(2,1)}, bf16[256,256]{1,0:T(8,128)(2,1)S(1)}, u32[]{:S(2)}, u32[]{:S(2)}) collective-permute-start(bf16[256,256]{1,0:T(8,128)(2,1)} %refs_14_), channel_id=1, source_target_pairs={{0,2},{2,0},{16,18},{18,16},{1,3},{3,1},{17,19},{19,17},{4,6},{6,4... | collective-permute-start | bytes 393224 | tf_op jit(solution)/shard_map/ppermute | solution.py:35
  50.1 11.4 %collective-permute-start.17 = (bf16[256,256]{1,0:T(8,128)(2,1)}, bf16[256,256]{1,0:T(8,128)(2,1)S(1)}, u32[]{:S(2)}, u32[]{:S(2)}) collective-permute-start(bf16[256,256]{1,0:T(8,128)(2,1)} %refs_14_), channel_id=1, source_target_pairs={{0,16},{2,18},{16,0},{18,2},{1,17},{3,19},{17,1},{19,3},{4,20},{6,... | collective-permute-start | bytes 393224 | tf_op jit(solution)/shard_map/ppermute | solution.py:35
  63.2 9.3 %collective-permute-start.22 = (bf16[256,256]{1,0:T(8,128)(2,1)S(1)}, bf16[256,256]{1,0:T(8,128)(2,1)S(1)}, u32[]{:S(2)}, u32[]{:S(2)}) collective-permute-start(bf16[256,256]{1,0:T(8,128)(2,1)S(1)} %collective-permute-done.18.refs_16_), channel_id=1, source_target_pairs={{0,1},{1,0},{2,3},{3,2},{4,5},{5,4},{6,7},{7,6},{8,9},{9,8},{10,11... | collective-permute-start | bytes 393224 | tf_op jit(solution)/shard_map/ppermute | solution.py:35
  63.2 9.2 %collective-permute-start.21 = (bf16[256,256]{1,0:T(8,128)(2,1)S(1)}, bf16[256,256]{1,0:T(8,128)(2,1)S(1)}, u32[]{:S(2)}, u32[]{:S(2)}) collective-permute-start(bf16[256,256]{1,0:T(8,128)(2,1)S(1)} %collective-permute-done.17.refs_15_), channel_id=1, source_target_pairs={{0,1},{1,0},{2,3},{3,2},{4,5},{5,4},{6,7},{7,6},{8,9},{9,8},{10,11... | collective-permute-start | bytes 393224 | tf_op jit(solution)/shard_map/ppermute | solution.py:35
  152.4 34.9 %all-to-all-start = ((bf16[16,5,64,128]{3,2,1,0:T(8,128)(2,1)}), bf16[16,5,64,128]{3,2,1,0:T(8,128)(2,1)}, u32[]{:S(2)}, u32[]{:S(2)}) async-start(bf16[16,5,64,128]{3,2,1,0:T(8,128)(2,1)} %shard_map.178), calls=%async_computation | async-start | bytes 2621440 | tf_op jit(solution)/shard_map/all_to_all | solution.py:602
  165.1 27.9 %collective-permute-start.41 = (bf16[528,256]{1,0:T(8,128)(2,1)}, bf16[528,256]{1,0:T(8,128)(2,1)}, u32[]{:S(2)}, u32[]{:S(2)}) collective-permute-start(bf16[528,256]{1,0:T(8,128)(2,1)} %get-tuple-element.118), channel_id=1, source_target_pairs={{0,16},{2,18},{16,0},{18,2},{1,17},{3,19},{17,1},{19,3},{4,20},{6,... | collective-permute-start | bytes 811016 | tf_op jit(solution)/shard_map/ppermute | solution.py:35
  165.1 28.0 %collective-permute-start.42 = (bf16[528,256]{1,0:T(8,128)(2,1)}, bf16[528,256]{1,0:T(8,128)(2,1)}, u32[]{:S(2)}, u32[]{:S(2)}) collective-permute-start(bf16[528,256]{1,0:T(8,128)(2,1)} %get-tuple-element.119), channel_id=1, source_target_pairs={{0,2},{2,0},{16,18},{18,16},{1,3},{3,1},{17,19},{19,17},{4,6},{6,4... | collective-permute-start | bytes 811016 | tf_op jit(solution)/shard_map/ppermute | solution.py:35
  169.5 28.9 %collective-permute-start.43 = (bf16[528,256]{1,0:T(8,128)(2,1)}, bf16[528,256]{1,0:T(8,128)(2,1)}, u32[]{:S(2)}, u32[]{:S(2)}) collective-permute-start(bf16[528,256]{1,0:T(8,128)(2,1)} %get-tuple-element.120), channel_id=1, source_target_pairs={{0,18},{2,16},{16,2},{18,0},{1,19},{3,17},{17,3},{19,1},{4,22},{6,... | collective-permute-start | bytes 811016 | tf_op jit(solution)/shard_map/ppermute | solution.py:35
  188.9 16.0 %collective-permute-start.47 = (bf16[64,128]{1,0:T(8,128)(2,1)S(1)}, bf16[64,128]{1,0:T(8,128)(2,1)S(1)}, u32[]{:S(2)}, u32[]{:S(2)}) collective-permute-start(bf16[64,128]{1,0:T(8,128)(2,1)S(1)} %get-tuple-element.160), channel_id=1, source_target_pairs={{0,6},{2,4},{4,14},{6,12},{8,22},{10,20},{12,30},{14,28},{16,2},{1... | collective-permute-start | bytes 49160 | tf_op jit(solution)/shard_map/ppermute | solution.py:35
  190.6 14.4 %collective-permute-start.46 = (bf16[64,128]{1,0:T(8,128)(2,1)S(1)}, bf16[64,128]{1,0:T(8,128)(2,1)S(1)}, u32[]{:S(2)}, u32[]{:S(2)}) collective-permute-start(bf16[64,128]{1,0:T(8,128)(2,1)S(1)} %get-tuple-element.161), channel_id=1, source_target_pairs={{0,2},{2,0},{4,10},{6,8},{8,18},{10,16},{12,26},{14,24},{16,6},{18... | collective-permute-start | bytes 49160 | tf_op jit(solution)/shard_map/ppermute | solution.py:35
  193.1 11.9 %collective-permute-start.45 = (bf16[64,128]{1,0:T(8,128)(2,1)S(1)}, bf16[64,128]{1,0:T(8,128)(2,1)S(1)}, u32[]{:S(2)}, u32[]{:S(2)}) collective-permute-start(bf16[64,128]{1,0:T(8,128)(2,1)S(1)} %get-tuple-element.162), channel_id=1, source_target_pairs={{0,4},{2,6},{4,12},{6,14},{8,20},{10,22},{12,28},{14,30},{16,0},{1... | collective-permute-start | bytes 49160 | tf_op jit(solution)/shard_map/ppermute | solution.py:35
  193.1 11.9 %collective-permute-start.44 = (bf16[64,128]{1,0:T(8,128)(2,1)S(1)}, bf16[64,128]{1,0:T(8,128)(2,1)S(1)}, u32[]{:S(2)}, u32[]{:S(2)}) collective-permute-start(bf16[64,128]{1,0:T(8,128)(2,1)S(1)} %get-tuple-element.163), channel_id=1, source_target_pairs={{0,0},{2,2},{4,8},{6,10},{8,16},{10,18},{12,24},{14,26},{16,4},{18... | collective-permute-start | bytes 49160 | tf_op jit(solution)/shard_map/ppermute | solution.py:35
  213.8 14.4 %collective-permute-start.52 = (bf16[2,5,16,128]{3,2,1,0:T(8,128)(2,1)S(1)}, bf16[2,5,16,128]{3,2,1,0:T(8,128)(2,1)S(1)}, u32[]{:S(2)}, u32[]{:S(2)}) collective-permute-start(bf16[2,5,16,128]{3,2,1,0:T(8,128)(2,1)S(1)} %bitcast.119), channel_id=1, source_target_pairs={{0,6},{2,4},{4,14},{6,12},{8,22},{10,20},{12,30},{14,28},{16,2},{1... | collective-permute-start | bytes 122888 | tf_op jit(solution)/shard_map/ppermute | solution.py:35
  213.8 14.3 %collective-permute-start.49 = (bf16[2,5,16,128]{3,2,1,0:T(8,128)(2,1)S(1)}, bf16[2,5,16,128]{3,2,1,0:T(8,128)(2,1)S(1)}, u32[]{:S(2)}, u32[]{:S(2)}) collective-permute-start(bf16[2,5,16,128]{3,2,1,0:T(8,128)(2,1)S(1)} %bitcast.117), channel_id=1, source_target_pairs={{0,0},{2,2},{4,8},{6,10},{8,16},{10,18},{12,24},{14,26},{16,4},{18... | collective-permute-start | bytes 122888 | tf_op jit(solution)/shard_map/ppermute | solution.py:35
  217.6 10.5 %collective-permute-start.51 = (bf16[2,5,16,128]{3,2,1,0:T(8,128)(2,1)S(1)}, bf16[2,5,16,128]{3,2,1,0:T(8,128)(2,1)S(1)}, u32[]{:S(2)}, u32[]{:S(2)}) collective-permute-start(bf16[2,5,16,128]{3,2,1,0:T(8,128)(2,1)S(1)} %bitcast.115), channel_id=1, source_target_pairs={{0,2},{2,0},{4,10},{6,8},{8,18},{10,16},{12,26},{14,24},{16,6},{18... | collective-permute-start | bytes 122888 | tf_op jit(solution)/shard_map/ppermute | solution.py:35
  224.5 10.2 %collective-permute-start.53 = (bf16[72,512]{1,0:T(8,128)(2,1)S(1)}, bf16[72,512]{1,0:T(8,128)(2,1)S(1)}, u32[]{:S(2)}, u32[]{:S(2)}) collective-permute-start(bf16[72,512]{1,0:T(8,128)(2,1)S(1)} %copy_bitcast_fusion.1), channel_id=1, source_target_pairs={{0,0},{2,64},{4,4},{6,68},{8,8},{10,72},{12,12},{14,76},{16,32},{1... | collective-permute-start | bytes 221192 | tf_op jit(solution)/shard_map/ppermute | solution.py:35
  (75 other events, 400.4 us)
Sparse Core Ops, SparseCore 0:
  18.5 49.0 all-gather.2
  101.6 87.7 reduce-scatter.1
where the time goes:
time: 243 us; the launch traced here: 242 us
  waiting for transfers between devices  73.1 us (30%)
  starting transfers between devices  71.9 us (30%)
  Pallas kernels  51.5 us (21%)
  local copies, waits for them, and re-layouts  25.5 us (10%)
  between operations  14.9 us (6%)
  other arithmetic  5.12 us (2%)
    ppermute x54, starting transfers between devices, moved(): return lax.ppermute(value, axes if len(axes) > 1 else axes[0], pairs)  59.2 us
    ppermute x54, waiting for transfers between devices, moved(): return lax.ppermute(value, axes if len(axes) > 1 else axes[0], pairs)  57 us
    pallas_call x10, Pallas kernels, call(): pl.pallas_call(body, out_shape=outs, in_specs=[pl.BlockSpec(memory_space=...  51.5 us
    all_to_all x1, waiting for transfers between devices, local(): late = lax.all_to_all(late, ('y', 'z'), 0, 0)  16.1 us
    all_to_all x1, starting transfers between devices, local(): late = lax.all_to_all(late, ('y', 'z'), 0, 0)  12.7 us
    unnamed x88, local copies, waits for them, and re-layouts  8.58 us
  transfers between devices with their start and end apart: 57, of which 21 were waited for; matrix products, arithmetic and copies ran while one was open for 8% of the time, Pallas kernels for 11%

commit v1 on v0

--- a/solution.py
+++ b/solution.py
@@ -97,7 +97,7 @@
 
 def front(place, *refs):
     near, far, w_own = refs[0:4], refs[4:8], refs[8]
-    x, n, gain, b, c, u, bx, tails, tail, same_one, same_two, w_far = refs[9:]
+    x, n, gain, b, c, u, bx, tails, tail, same_one, same_two, scale, w_far = refs[9:]
     row, xl, col = place[0], place[1], place[2]
     assemble(x, row, col, near, far)
     for k in (0, 2):
@@ -116,7 +116,9 @@
     @pl.loop(0, 8)
     def _(i):
         v = x[rows(i, 64)].astype(f32)
-        n[rows(i, 64)] = (v * norm_scale(v) * gain[0:1]).astype(low)
+        r = norm_scale(v)
+        scale[rows(i, 64)] = jnp.broadcast_to(r, (64, 128))
+        n[rows(i, 64)] = (v * r * gain[0:1]).astype(low)
 
     for i in range(3):
         for e in (0, 1):
@@ -218,19 +220,28 @@
         send[k, :256] = wide[here, lanes(2 * (k >> 1) + 1 - col, 256)].astype(low)
 
 
-def feed_weights(place, n, act, dgate, dup, df, down_own, down_far, early, keep, send, wide):
-    row, xl, col = place[0], place[1], place[2]
+def feed_out(place, act, down_own, down_far, keep, send, wide):
     for k, w in ((0, down_own), (1, down_far)):
-        wide[:512, 512 * k : 512 * k + 512] = mm(act[...], w[...])
-    part(wide, keep, send, col)
+        wide[:, 512 * k : 512 * k + 512] = mm(act[...], w[...])
+    part(wide, keep, send, place[2])
+
+
+def source_row(m, half):
+    return 128 * (m // 4) + 64 * half + 16 * (m % 4)
+
+
+def feed_weights(place, n, act, dgate, dup, df, early, wide):
+    xl = place[1]
     n_t = n[...].T
     for k, g in ((0, dgate), (1, dup)):
         for r in (0, 1):
             total = mm(n_t[512 * r : 512 * r + 512], g[...]).astype(low)
             for m in range(16):
                 for t in range(5):
-                    at = ((r * 2 + k) * 5 + t) * 32
-                    early[m, at : at + 32] = total[32 * m : 32 * m + 32, 128 * t : 128 * t + 128]
+                    for h in (0, 1):
+                        at = ((r * 2 + k) * 5 + t) * 32 + 16 * h
+                        first = source_row(m, h)
+                        early[m, at : at + 16] = total[first : first + 16, 128 * t : 128 * t + 128]
     wide[...] = mm(act[...].T, df[...])
     for i in range(8):
         some = wide[pl.ds(pl.multiple_of(64 * xl + 72 * i, 8), 72)]
@@ -290,9 +301,10 @@
 
 def conv_backward(place, *refs):
     dconv, dc, later, last, same_one, same_two, taps, b, c, u, past_one, past_two, bx, w_own, w_far = refs[:15]
-    dproj, keep, send, total, grad_conv = refs[15:20]
-    (wide,) = refs[20:]
-    xl, col, zz = place[1], place[2], place[4]
+    x, scale, dg_two = refs[15:18]
+    dproj, keep, send, total, small = refs[18:23]
+    (wide,) = refs[23:]
+    row, xl, col, zz = place[0], place[1], place[2], place[4]
     end = zz == 3
     rim = jnp.where(end, later[1], later[0]), jnp.where(end, last[...], later[1])
     parts = []
@@ -325,10 +337,25 @@
         both = jnp.concatenate([high, rest])
         send[i, 256:272] = both
         send[2 + i, 256:272] = both
-    grad_conv[...] = parts[0] + parts[1]
+    zero = jnp.zeros((1, 128), f32)
     for k, w in ((0, w_own), (1, w_far)):
         whole = jnp.concatenate([w[0], w[1], w[2]], axis=1)
         wide[:, 512 * k : 512 * k + 512] = mm_t(dproj[...], whole)
+        sums = jnp.zeros((1, 512), f32)
+        for i in range(8):
+            here = slice(64 * i, 64 * i + 64)
+            v = x[here, lanes(row ^ k, 512)].astype(f32)
+            r = scale[here]
+            r = jnp.concatenate([r, r, r, r], axis=1)
+            sums += jnp.sum(wide[here, 512 * k : 512 * k + 512] * v * r, axis=0, keepdims=True)
+        lines = [sums[:, 128 * t : 128 * t + 128] for t in range(4)]
+        if k == 0:
+            lines += [dg_two[0:1, :128], dg_two[0:1, 128:]]
+            for a in range(3):
+                tap = parts[0][a : a + 1] + parts[1][a : a + 1]
+                lines += [jnp.where(xl == 0, tap, zero), jnp.where(xl == 0, zero, tap)]
+        lines += [zero] * (16 - len(lines))
+        small[row ^ k] = jnp.concatenate(lines).astype(low)
     part(wide, keep, send, col)
 
 
@@ -339,9 +366,8 @@
         for m in range(16):
             for h in (0, 1):
                 for k in range(3):
-                    late[m, 2 * r + h, 16 * k : 16 * k + 16] = total[
-                        32 * m + 16 * h : 32 * m + 16 * h + 16, 128 * k : 128 * k + 128
-                    ]
+                    first = source_row(m, h)
+                    late[m, 2 * r + h, 16 * k : 16 * k + 16] = total[first : first + 16, 128 * k : 128 * k + 128]
                 late[m, 2 * r + h, 48:64] = small[r]
     total = mm(y[...].T, do[...]).astype(low)
     for r in (0, 1):
@@ -352,11 +378,7 @@
                 ]
 
 
-def fold_last(place, keep, got, keep_ffn, got_ffn, total, x, dg_two, grad_conv, own, own_ffn, mass, *rest):
-    others, small = rest[:3], rest[3]
-    row, xl, col = place[0], place[1], place[2]
-    sums = [jnp.zeros((1, 256), f32), jnp.zeros((1, 256), f32)]
-    scale = norm_scale(x[...].astype(f32))
+def fold_last(place, keep, got, keep_ffn, got_ffn, total, own, own_ffn, mass, *others):
     for k in range(4):
         whole = keep[k] + got[k, :256].astype(f32)
         line = total[k & 1] + got[k, 256:264].astype(f32) + got[k, 264:272].astype(f32)
@@ -370,17 +392,6 @@
             others[k - 1][:256] = whole.astype(low)
             high = line.astype(low)
             others[k - 1][256:272] = jnp.concatenate([high, (line - high.astype(f32)).astype(low)])
-        at = (k & 1) * 256
-        v = x[at : at + 256, lanes((row ^ (k >> 1)) * 2 + col, 256)].astype(f32)
-        sums[k >> 1] += jnp.sum(whole * v * scale[at : at + 256], axis=0, keepdims=True)
-    zero = jnp.zeros((1, 128), f32)
-    pair = lambda v: [v[:, :128], v[:, 128:]]
-    taps = []
-    for a in range(3):
-        w = grad_conv[a : a + 1]
-        taps += [jnp.where(xl == 0, w, zero), jnp.where(xl == 0, zero, w)]
-    small[row] = jnp.concatenate(pair(sums[0]) + pair(dg_two[0:1]) + taps + [zero] * 6).astype(low)
-    small[1 - row] = jnp.concatenate(pair(sums[1]) + [zero] * 14).astype(low)
 
 
 def finish(place, own, own_ffn, mass, got1, got2, got3, dh, hidden, x, gain, out, mixed):
@@ -397,6 +408,60 @@
     v = x[:256, here].astype(f32)
     mixed[...] = (hidden[...] + ffn).astype(low)
     out[...] = (dh[...] + scale * gain[0:1, here] * total - v * (scale * scale) * column / 1024).astype(low)
+
+
+def deal(place, late, early, settled, *messages):
+    row, xl = place[0], place[1]
+
+    def total(block, here):
+        parts = [late[m, block, here].astype(f32) for m in range(16)]
+        while len(parts) > 1:
+            parts = [a + b for a, b in zip(parts[::2], parts[1::2])]
+        return parts[0].astype(low)
+
+    for j, message in enumerate(messages):
+        r, half = row ^ (j >> 1), xl ^ (j & 1)
+        message[0:64] = total(2 * r + half, slice(None))
+        for i in range(10):
+            message[64 + 16 * i : 80 + 16 * i] = early[pl.ds(pl.multiple_of((10 * r + i) * 32 + 16 * half, 16), 16)]
+    settled[0:64] = total(4, slice(None))
+    settled[64:384] = early[640:960]
+
+
+def place_out(place, settled, m0, m1, m2, m3, g_in, g_out, g_gu, g_down, small, cross):
+    row, xl, col = place[0], place[1], place[2]
+    spot = 2 * row + xl
+    got = (m0, m1, m2, m3)
+
+    def sender(q, here):
+        return jnp.where(
+            spot == q,
+            got[0][here],
+            jnp.where(spot == (q ^ 1), got[1][here], jnp.where(spot == (q ^ 2), got[2][here], got[3][here])),
+        ).astype(f32)
+
+    extra = jnp.zeros((16, 128), f32)
+    for q in range(4):
+        whole = sender(q, slice(None))
+        for k in range(3):
+            g_in[k, :, 128 * q : 128 * q + 128] = whole[16 * k : 16 * k + 16]
+        extra += whole[48:64]
+        first = 9 * q // 2
+        for k in (0, 1):
+            for t in range(5):
+                at = 64 + 16 * (5 * k + t)
+                here = slice(128 * (first + t), 128 * (first + t) + 128)
+                if q % 2 and t == 0:
+                    g_gu[:, k, here] += whole[at : at + 16]
+                else:
+                    g_gu[:, k, here] = whole[at : at + 16]
+    swap = col == 1
+    small[...] = jnp.concatenate([jnp.where(swap, extra[2:4], extra[0:2]), extra[4:]], axis=0)
+    cross[...] = jnp.concatenate([jnp.where(swap, extra[0:2], extra[2:4]), extra[:6]], axis=0)
+    for t in range(4):
+        here = slice(128 * t, 128 * t + 128)
+        g_out[:, here] = settled[16 * t : 16 * t + 16].astype(f32)
+        g_down[:, here] = settled[64 + 80 * t : 144 + 80 * t].astype(f32)[:72]
 
 
 def local(
@@ -434,7 +499,6 @@
     in_own, in_send = cut(in_w, q, 128, 2), cut(in_w, 3 - q, 128, 2)
     in_send = jnp.concatenate([in_send[:, :256], in_send[:, 256:]], axis=2).reshape(768, 256)
     near = [piece, ring(piece, 1), ring(piece, 2), ring(jnp.concatenate([piece, in_send]), 3)]
-    far = [swap_core(v) for v in near[:3]] + [swap_core(near[3][:272])]
     taps = jnp.pad(cut(conv_weight, xl, 128, 0).T.astype(f32), ((0, 5), (0, 0)))
 
     def begin(index):
@@ -452,12 +516,30 @@
     out_swap = swap_core(out_weight)
     gu_own, down_own = window(gate_up.transpose(1, 0, 2), q, 2), window(down_weight, q, 0)
 
+    out_line = cut(out_weight, q, 128, 0)
+    in_own, gu_own, down_own, taps, out_line, place, near[1] = lax.optimization_barrier(
+        (in_own, gu_own, down_own, taps, out_line, place, near[1])
+    )
+    far = [swap_core(v) for v in near[:3]] + [swap_core(near[3][:272])]
     tile = shaped(512, 128)
     tile_low = shaped(512, 128, kind=low)
     whole_low = shaped(512, 1024, kind=low)
-    x, n_one, gain, b, c, u, bx, tails, tail, same_one, same_two = call(
+    x, n_one, gain, b, c, u, bx, tails, tail, same_one, same_two, scale = call(
         front,
-        [whole_low, whole_low, shaped(16, 1024), tile, tile, tile, tile_low, shaped(2, 8, 128), shaped(8, 128), tile, tile],
+        [
+            whole_low,
+            whole_low,
+            shaped(16, 1024),
+            tile,
+            tile,
+            tile,
+            tile_low,
+            shaped(2, 8, 128),
+            shaped(8, 128),
+            tile,
+            tile,
+            tile,
+        ],
         [pltpu.VMEM((3, 512, 128), low)],
         place,
         *near,
@@ -520,10 +602,9 @@
     own_low = shaped(256, 256, kind=low)
     dn_own, *parts = call(fold, [own, own_low, own_low, own_low], [], place, keep, got)
     ringed = [ring(v, k) for k, v in zip((1, 2, 3), parts)]
-    n_two, dn_own, *parts = lax.optimization_barrier((n_two, dn_own, *parts))
-    early, keep_ffn, send_ffn = call(
+    (early,) = call(
         feed_weights,
-        [shaped(16, 960, 128, kind=low), keep4, send4],
+        [shaped(16, 960, 128, kind=low)],
         [pltpu.VMEM((640, 1024), f32)],
         place,
         n_two,
@@ -531,13 +612,10 @@
         dgate,
         dup,
         df,
-        down_own,
-        down_far,
     )
     dn_own, early = lax.optimization_barrier((dn_own, early))
     early = early.reshape(16 * 960, 128)
     early = lax.psum_scatter(early, ("y", "z"), scatter_dimension=0, tiled=True)
-    got_ffn = swap_core(send_ffn)
     piece = (dn_own + sum(v.astype(f32) for v in ringed)).astype(low)
     near = [piece] + [ring(piece, k) for k in (1, 2, 3)]
     far = [swap_core(v) for v in near]
@@ -551,18 +629,24 @@
         hidden,
         df,
         gain,
-        cut(out_weight, q, 128, 0),
+        out_line,
         out_row,
         c,
         conv,
         same_one,
         same_two,
     )
+    act, heads = lax.optimization_barrier((act, heads))
+    keep_ffn, send_ffn = call(
+        feed_out, [keep4, send4], [pltpu.VMEM((512, 1024), f32)], place, act, down_own, down_far
+    )
+    dconv, send_ffn = lax.optimization_barrier((dconv, send_ffn))
+    got_ffn = swap_core(send_ffn)
     later = moved(heads, ("z",), lambda z: ((z - 1) % 4,))
     last = moved(head, ("y", "z"), lambda y, z: (y - 1, 3) if z == 0 and y > 0 else None)
-    dproj, keep, send, total, grad_conv = call(
+    dproj, keep, send, total, small = call(
         conv_backward,
-        [shaped(512, 384, kind=low), keep4, send4_mass, shaped(2, 8, 256), shaped(8, 128)],
+        [shaped(512, 384, kind=low), keep4, send4_mass, shaped(2, 8, 256), shaped(2, 16, 128, kind=low)],
         [pltpu.VMEM((512, 1024), f32)],
         place,
         dconv,
@@ -580,12 +664,15 @@
         bx,
         in_own,
         in_far,
+        x,
+        scale,
+        dg_two,
     )
     got = swap_core(send)
     own_mass = shaped(528, 256, kind=low)
-    dn_own, ffn_own, mass, *parts, small = call(
+    dn_own, ffn_own, mass, *parts = call(
         fold_last,
-        [own, own, shaped(8, 256), own_mass, own_mass, own_mass, shaped(2, 16, 128, kind=low)],
+        [own, own, shaped(8, 256), own_mass, own_mass, own_mass],
         [],
         place,
         keep,
@@ -593,9 +680,6 @@
         keep_ffn,
         got_ffn,
         total,
-        x,
-        dg_two,
-        grad_conv,
     )
     (late,) = call(mix_weights, [shaped(16, 5, 64, 128, kind=low)], [], place, n_one, dproj, y, do, small)
     ringed = [ring(v, k) for k, v in zip((1, 2, 3), parts)]
@@ -605,59 +689,38 @@
         finish, [own_low, own_low], [], place, dn_own, ffn_own, mass, *ringed, dh_own, h_own, x, gain
     )
 
-    def settle(value):
-        return moved(
-            value,
-            ("y", "xl", "z", "row"),
-            lambda y, xl, z, r: (2 * r + xl, y % 2, z, y // 2),
-        ).astype(f32)
-
-    spot = 2 * row + zz % 2
-
-    def spread(pick):
-        got = jnp.stack(
-            [
-                moved(
-                    pick(row ^ (j >> 1), xl ^ (j & 1)),
-                    ("y", "xl", "z", "row"),
-                    lambda y, xl, z, r, j=j: (y, z // 2, 2 * (z % 2) + (xl ^ (j & 1)), r ^ (j >> 1)),
-                )
-                for j in range(4)
-            ]
-        )
-        return [lax.dynamic_index_in_dim(got, spot ^ k, 0, keepdims=False) for k in range(4)]
-
-    gu_early = early[:640].reshape(2, 10, 2, 16, 128)
-    down_early = early[640:].reshape(4, 80, 128)[:, :72].transpose(1, 0, 2).reshape(72, 512)
-    gu_got = spread(lambda r, half: lax.dynamic_slice(gu_early, (r, 0, half, 0, 0), (1, 10, 1, 16, 128)).reshape(2, 5, 16, 128))
-    gu_got = [w.astype(f32) for w in gu_got]
-    grad_gate_up = jnp.concatenate(
+    late, grad_tokens, mixed = lax.optimization_barrier((late, grad_tokens, mixed))
+
+    settled, *messages = call(
+        deal, [shaped(384, 128, kind=low)] + [shaped(224, 128, kind=low)] * 4, [], place, late, early
+    )
+    settled = moved(
+        settled, ("y", "xl", "z", "row"), lambda y, xl, z, r: (2 * r + xl, y % 2, z, y // 2)
+    )
+    messages = [messages[0]] + [ring(messages[k], k) for k in (1, 2, 3)]
+    grad_in, grad_out, grad_gate_up, grad_down, small, cross = call(
+        place_out,
         [
-            gu_got[0][:, :4],
-            gu_got[0][:, 4:] + gu_got[1][:, :1],
-            gu_got[1][:, 1:],
-            gu_got[2][:, :4],
-            gu_got[2][:, 4:] + gu_got[3][:, :1],
-            gu_got[3][:, 1:],
+            shaped(3, 16, 512),
+            shaped(16, 512),
+            shaped(16, 2, 2304),
+            shaped(72, 512),
+            shaped(14, 128),
+            shaped(8, 128),
         ],
-        axis=1,
-    )
-    grad_gate_up = grad_gate_up.transpose(2, 0, 1, 3).reshape(16, 2, 2304)
-    grad_down = settle(down_early)
-
-    late = jnp.sum(late.astype(f32), axis=0).astype(low)
-    grad_out = settle(late[4].reshape(4, 16, 128).transpose(1, 0, 2).reshape(16, 512))
-    in_got = spread(lambda r, half: lax.dynamic_index_in_dim(late, 2 * r + half, 0, keepdims=False))
-    grad_in = jnp.concatenate(
-        [w[:48].reshape(3, 16, 128).transpose(1, 0, 2) for w in in_got], axis=-1
-    ).astype(f32)
-    small = sum(w[48:].astype(f32) for w in in_got)[:10].reshape(5, 256)
+        [],
+        place,
+        settled,
+        *messages,
+    )
+    cross = swap_core(cross)
+    small = jnp.concatenate([small[:2] + cross[:2], small[2:10]]).reshape(5, 256)
     small = cut(small, 8 * yy + 4 * xl + zz, 8, 1)
     return (
         mixed,
         grad_tokens,
         small[0],
-        grad_in,
+        grad_in.transpose(1, 0, 2),
         small[2:5].T,
         grad_out,
         small[1],

time: 243 us -> 212 us (0.87)
  the two profiles are of different devices: /device:TPU:38 before, /device:TPU:1 now
where the time goes in v1:
time: 212 us; the launch traced here: 211 us
  starting transfers between devices  65 us (31%)
  Pallas kernels  57.6 us (27%)
  waiting for transfers between devices  46.3 us (22%)
  local copies, waits for them, and re-layouts  24.7 us (12%)
  between operations  14.7 us (7%)
  other arithmetic  2.98 us (1%)
    ppermute x49, starting transfers between devices, moved(): return lax.ppermute(value, axes if len(axes) > 1 else axes[0], pairs)  59.4 us
    pallas_call x13, Pallas kernels, call(): pl.pallas_call(body, out_shape=outs, in_specs=[pl.BlockSpec(memory_space=...  57.6 us
    ppermute x49, waiting for transfers between devices, moved(): return lax.ppermute(value, axes if len(axes) > 1 else axes[0], pairs)  46.2 us
    unnamed x109, local copies, waits for them, and re-layouts  10.2 us
    all_to_all x1, starting transfers between devices, local(): late = lax.all_to_all(late, ('y', 'z'), 0, 0)  5.56 us
  transfers between devices with their start and end apart: 52, of which 20 were waited for; matrix products, arithmetic and copies ran while one was open for 7% of the time, Pallas kernels for 17%

profile of v1, /device:TPU:1, one launch (start us, length us, event | category | flops | bytes accessed | tf_op | source)
XLA Modules:
  0.0 211.3 jit_solution(12770410702392945210)
XLA Ops:
  10.2 3.4 %collective-permute-start.24 = (bf16[640,128]{1,0:T(8,128)(2,1)S(1)}, bf16[640,128]{1,0:T(8,128)(2,1)S(1)}, u32[]{:S(2)}, u32[]{:S(2)}) collective-permute-start(bf16[640,128]{1,0:T(8,128)(2,1)S(1)} %pad_maximum_fusion.3), channel_id=1, source_target_pairs={{0,18},{2,16},{16,2},{18,0},{1,19},{3,17},{17,3},{19,1},{4,22},{6,... | collective-permute-start | bytes 491528 | tf_op jit(solution)/shard_map/ppermute | solution.py:35
  14.5 4.4 %collective-permute-done.25 = bf16[128,128]{1,0:T(8,128)(2,1)S(1)} collective-permute-done((bf16[128,128]{1,0:T(8,128)(2,1)S(1)}, bf16[128,128]{1,0:T(8,128)(2,1)S(1)}, u32[]{:S(2)}, u32[]{:S(2)}) %collective-permute-start.25) | collective-permute-done | bytes 32800 | tf_op jit(solution)/shard_map/ppermute | solution.py:35
  27.9 3.3 %constant_dynamic-slice_fusion.8 = bf16[512,2,640]{2,1,0:T(2,128)(2,1)} fusion(bf16[512,2,2304]{2,1,0:T(2,128)(2,1)} %param.17, s32[]{:T(128)S(6)} %select_n.45), kind=kLoop, calls=%fused_computation.18 | loop fusion | bytes 2621444 | tf_op jit(solution)/shard_map/dynamic-slice.1
  36.6 5.6 %collective-permute-done.2.refs_3_ = bf16[1040,256]{1,0:T(8,128)(2,1)S(1)} collective-permute-done((bf16[1040,256]{1,0:T(8,128)(2,1)}, bf16[1040,256]{1,0:T(8,128)(2,1)S(1)}, u32[]{:S(2)}, u32[]{:S(2)}) %collective-permute-start.2) | collective-permute-done | bytes 532512 | tf_op jit(solution)/shard_map/ppermute | solution.py:35
  44.7 4.7 %shard_map.169 = (bf16[512,1024]{1,0:T(8,128)(2,1)}, bf16[512,1024]{1,0:T(8,128)(2,1)}, f32[16,1024]{1,0:T(8,128)}, f32[512,128]{1,0:T(8,128)}, f32[512,128]{1,0...) custom-call(s32[5]{0:T(128)} %stack.55.place, ...), custom_call_target="tpu_custom_call" | custom-call | tf_op jit(solution)/shard_map/pallas_call | solution.py:72
  58.8 2.7 %collective-permute-done.19.refs_17_ = bf16[256,256]{1,0:T(8,128)(2,1)S(1)} collective-permute-done((bf16[256,256]{1,0:T(8,128)(2,1)S(1)}, bf16[256,256]{1,0:T(8,128)(2,1)S(1)}, u32[]{:S(2)}, u32[]{:S(2)}) %collective-permute-start.19) | collective-permute-done | bytes 131104 | tf_op jit(solution)/shard_map/ppermute | solution.py:35
  71.9 14.4 %shard_map.171 = (f32[512,1024]{1,0:T(8,128)}, bf16[512,1024]{1,0:T(8,128)(2,1)}, bf16[512,640]{1,0:T(8,128)(2,1)}, bf16[512,640]{1,0:T(8,128)(2,1)}, bf16[512,6...) custom-call(s32[5]{0:T(128)} %stack.55.place, ...), custom_call_target="tpu_custom_call" | custom-call | tf_op jit(solution)/shard_map/pallas_call | solution.py:72
  86.7 6.7 %shard_map.173 = bf16[16,960,128]{2,1,0:T(8,128)(2,1)} custom-call(s32[5]{0:T(128)} %stack.55.place, bf16[512,1024]{1,0:T(8,128)(2,1)} %get-tuple-element.113.n, bf16[512,640]{1,0:T(8,128)(2,1)} %get-tuple-element.128.act, bf16[512,640]{1,0:T(8,128)(2,1)} %get-tuple-element.115.dgate, bf16[512,640]{1,0:T(8,128)(2,1)} %get-tuple-element.116.dup, ...), custom_call_target="tpu_custom_call" | custom-call | tf_op jit(solution)/shard_map/pallas_call | solution.py:72
  102.3 3.6 %collective-permute-done.28 = bf16[256,256]{1,0:T(8,128)(2,1)S(1)} collective-permute-done((bf16[256,256]{1,0:T(8,128)(2,1)S(1)}, bf16[256,256]{1,0:T(8,128)(2,1)S(1)}, u32[]{:S(2)}, u32[]{:S(2)}) %collective-permute-start.28) | collective-permute-done | bytes 131104 | tf_op jit(solution)/shard_map/ppermute | solution.py:35
  113.5 4.0 %collective-permute-start.36 = (bf16[256,256]{1,0:T(8,128)(2,1)S(1)}, bf16[256,256]{1,0:T(8,128)(2,1)S(1)}, u32[]{:S(2)}, u32[]{:S(2)}) collective-permute-start(bf16[256,256]{1,0:T(8,128)(2,1)S(1)} %collective-permute-done.32.refs_3_), channel_id=1, source_target_pairs={{0,1},{1,0},{2,3},{3,2},{4,5},{5,4},{6,7},{7,6},{8,9},{9,8},{10,11... | collective-permute-start | bytes 393224 | tf_op jit(solution)/shard_map/ppermute | solution.py:35
  121.0 5.5 %shard_map.174 = (f32[256,256]{1,0:T(8,128)}, bf16[512,1024]{1,0:T(8,128)(2,1)}, f32[512,128]{1,0:T(8,128)}, f32[512,128]{1,0:T(8,128)}, f32[2,16,128]{2,1,0:T(8...) custom-call(s32[5]{0:T(128)} %stack.55.place, bf16[256,256]{1,0:T(8,128)(2,1)} %copy-done.6, bf16[256,256]{1,0:T(8,128)(2,1)} %copy-done.32, ...), custom_call_target="tpu_custom_call" | custom-call | tf_op jit(solution)/shard_map/pallas_call | solution.py:72
  126.6 5.4 %collective-permute-start.37 = (f32[2,16,128]{2,1,0:T(8,128)}, f32[2,16,128]{2,1,0:T(8,128)S(1)}, u32[]{:S(2)}, u32[]{:S(2)}) collective-permute-start(f32[2,16,128]{2,1,0:T(8,128)} %get-tuple-element.133), channel_id=1, source_target_pairs={{0,12},{4,0},{8,4},{12,8},{1,13},{5,1},{9,5},{13,9},{2,14},{6,2},{... | collective-permute-start | bytes 49160 | tf_op jit(solution)/shard_map/ppermute | solution.py:35
  133.8 3.8 %shard_map.175 = (f32[4,256,256]{2,1,0:T(8,128)}, bf16[4,256,256]{2,1,0:T(8,128)(2,1)}) custom-call(s32[5]{0:T(128)} %stack.55.place, bf16[512,640]{1,0:T(8,128)(2,1)} %get-tuple-element.128.act, bf16[640,512]{1,0:T(8,128)(2,1)} %constant_dynamic-slice_fusion.7.refs_13_.down_own, bf16[640,512]{1,0:T(8,128)(2,1)} %get-tuple-element.129.down_far), custom_call_target="tpu_custom_call" | custom-call | tf_op jit(solution)/shard_map/pallas_call | solution.py:72
  138.2 4.3 %shard_map.176 = (bf16[512,384]{1,0:T(8,128)(2,1)}, f32[4,256,256]{2,1,0:T(8,128)}, bf16[4,272,256]{2,1,0:T(8,128)(2,1)}, f32[2,8,256]{2,1,0:T(8,128)}, bf16[2,16,128]{2,1,0:T(8,128)(2,1)}) custom-call(s32[5]{0:T(128)} %stack.55.place, f32[512,128]{1,0:T(8,128)} %get-tuple-element.131.refs_0_, f32[512,128]{1,0:T(8,128)} %get-tuple-element.132.refs_1_, ...), custom_call_target="tpu_custom_call" | custom-call | tf_op jit(solution)/shard_map/pallas_call | solution.py:72
  142.6 3.7 %shard_map.177 = bf16[16,5,64,128]{3,2,1,0:T(8,128)(2,1)} custom-call(s32[5]{0:T(128)} %stack.55.place, bf16[512,1024]{1,0:T(8,128)(2,1)} %get-tuple-element.94.n, bf16[512,384]{1,0:T(8,128)(2,1)} %get-tuple-element.141.dproj, bf16[512,128]{1,0:T(8,128)(2,1)} %get-tuple-element.103.refs_0_.y, bf16[512,1024]{1,0:T(8,128)(2,1)} %get-tuple-element.142.do, ...), custom_call_target="tpu_custom_call" | custom-call | tf_op jit(solution)/shard_map/pallas_call | solution.py:72
  146.2 5.6 %all-to-all-start = ((bf16[16,5,64,128]{3,2,1,0:T(8,128)(2,1)}), bf16[16,5,64,128]{3,2,1,0:T(8,128)(2,1)}, u32[]{:S(2)}, u32[]{:S(2)}) async-start(bf16[16,5,64,128]{3,2,1,0:T(8,128)(2,1)} %shard_map.177), calls=%async_computation | async-start | bytes 2621440 | tf_op jit(solution)/shard_map/all_to_all | solution.py:686
  156.3 3.0 %shard_map.178 = (f32[256,256]{1,0:T(8,128)}, f32[256,256]{1,0:T(8,128)}, f32[8,256]{1,0:T(8,128)}, bf16[528,256]{1,0:T(8,128)(2,1)}, bf16[528,256]{1,0:T(8,128)(2,1)}, /*index=5*/bf16[528,256]{1,0:T(8,128)(2,1)}) custom-call(s32[5]{0:T(128)} %stack.55.place, f32[4,256,256]{2,1,0:T(8,128)} %get-tuple-element.144.keep, bf16[4,272,256]{2,1,0:T(8,128)(2,1)} %copy-done.4, ...), custom_call_target="tpu_custom_call" | custom-call | tf_op jit(solution)/shard_map/pallas_call | solution.py:72
  159.3 2.8 %collective-permute-start.42 = (bf16[528,256]{1,0:T(8,128)(2,1)}, bf16[528,256]{1,0:T(8,128)(2,1)S(1)}, u32[]{:S(2)}, u32[]{:S(2)}) collective-permute-start(bf16[528,256]{1,0:T(8,128)(2,1)} %get-tuple-element.153), channel_id=1, source_target_pairs={{0,2},{2,0},{16,18},{18,16},{1,3},{3,1},{17,19},{19,17},{4,6},{6,4... | collective-permute-start | bytes 811016 | tf_op jit(solution)/shard_map/ppermute | solution.py:35
  167.3 7.1 %collective-permute-done.42.got2 = bf16[528,256]{1,0:T(8,128)(2,1)S(1)} collective-permute-done((bf16[528,256]{1,0:T(8,128)(2,1)}, bf16[528,256]{1,0:T(8,128)(2,1)S(1)}, u32[]{:S(2)}, u32[]{:S(2)}) %collective-permute-start.42) | collective-permute-done | bytes 270368 | tf_op jit(solution)/shard_map/ppermute | solution.py:35
  177.2 2.8 %shard_map.179 = (bf16[256,256]{1,0:T(8,128)(2,1)}, bf16[256,256]{1,0:T(8,128)(2,1)}) custom-call(s32[5]{0:T(128)} %stack.55.place, f32[256,256]{1,0:T(8,128)} %get-tuple-element.149.own, f32[256,256]{1,0:T(8,128)} %get-tuple-element.150.own_ffn, f32[8,256]{1,0:T(8,128)} %get-tuple-element.151.mass, bf16[528,256]{1,0:T(8,128)(2,1)} %copy-done.9, ...), custom_call_target="tpu_custom_call" | custom-call | tf_op jit(solution)/shard_map/pallas_call | solution.py:72
  183.8 3.1 %collective-permute-start.45 = (bf16[224,128]{1,0:T(8,128)(2,1)}, bf16[224,128]{1,0:T(8,128)(2,1)S(1)}, u32[]{:S(2)}, u32[]{:S(2)}) collective-permute-start(bf16[224,128]{1,0:T(8,128)(2,1)} %get-tuple-element.164), channel_id=1, source_target_pairs={{0,16},{2,18},{16,0},{18,2},{1,17},{3,19},{17,1},{19,3},{4,20},{6,... | collective-permute-start | bytes 172040 | tf_op jit(solution)/shard_map/ppermute | solution.py:35
  186.9 3.6 %collective-permute-start.46 = (bf16[224,128]{1,0:T(8,128)(2,1)}, bf16[224,128]{1,0:T(8,128)(2,1)S(1)}, u32[]{:S(2)}, u32[]{:S(2)}) collective-permute-start(bf16[224,128]{1,0:T(8,128)(2,1)} %get-tuple-element.165), channel_id=1, source_target_pairs={{0,2},{2,0},{16,18},{18,16},{1,3},{3,1},{17,19},{19,17},{4,6},{6,4... | collective-permute-start | bytes 172040 | tf_op jit(solution)/shard_map/ppermute | solution.py:35
  190.5 2.8 %collective-permute-done.46.m2 = bf16[224,128]{1,0:T(8,128)(2,1)S(1)} collective-permute-done((bf16[224,128]{1,0:T(8,128)(2,1)}, bf16[224,128]{1,0:T(8,128)(2,1)S(1)}, u32[]{:S(2)}, u32[]{:S(2)}) %collective-permute-start.46) | collective-permute-done | bytes 57376 | tf_op jit(solution)/shard_map/ppermute | solution.py:35
  193.3 2.9 %collective-permute-done.47.m3 = bf16[224,128]{1,0:T(8,128)(2,1)S(1)} collective-permute-done((bf16[224,128]{1,0:T(8,128)(2,1)}, bf16[224,128]{1,0:T(8,128)(2,1)S(1)}, u32[]{:S(2)}, u32[]{:S(2)}) %collective-permute-start.47) | collective-permute-done | bytes 57376 | tf_op jit(solution)/shard_map/ppermute | solution.py:35
  (254 shorter events, 87.4 us)
Async XLA Ops:
  7.2 64.6 %all-gather.3.cloned.1.call-start = ((), (), s32[]{:S(2)}) async-start(), calls=%async_computation.3 | async-start | bytes 3342336 | tf_op jit(solution)/shard_map/all_gather | solution.py:515
  10.2 8.8 %collective-permute-start.24 = (bf16[640,128]{1,0:T(8,128)(2,1)S(1)}, bf16[640,128]{1,0:T(8,128)(2,1)S(1)}, u32[]{:S(2)}, u32[]{:S(2)}) collective-permute-start(bf16[640,128]{1,0:T(8,128)(2,1)S(1)} %pad_maximum_fusion.3), channel_id=1, source_target_pairs={{0,18},{2,16},{16,2},{18,0},{1,19},{3,17},{17,3},{19,1},{4,22},{6,... | collective-permute-start | bytes 491528 | tf_op jit(solution)/shard_map/ppermute | solution.py:35
  19.7 160.4 %reduce-scatter.2.cloned.1.call-start = ((), (), s32[]{:S(2)}) async-start(), calls=%async_computation.2 | async-start | bytes 4177920 | tf_op jit(solution)/shard_map/reduce_scatter | solution.py:618
  19.9 23.1 %collective-permute-start.3 = (bf16[272,256]{1,0:T(8,128)(2,1)S(1)}, bf16[272,256]{1,0:T(8,128)(2,1)}, u32[]{:S(2)}, u32[]{:S(2)}) collective-permute-start(bf16[272,256]{1,0:T(8,128)(2,1)S(1)} %pad_maximum_fusion.4.refs_0_), channel_id=1, source_target_pairs={{0,1},{1,0},{2,3},{3,2},{4,5},{5,4},{6,7},{7,6},{8,9},{9,8},{10,11... | collective-permute-start | bytes 417800 | tf_op jit(solution)/shard_map/ppermute | solution.py:35
  20.5 15.9 %collective-permute-start.1 = (bf16[272,256]{1,0:T(8,128)(2,1)S(1)}, bf16[272,256]{1,0:T(8,128)(2,1)}, u32[]{:S(2)}, u32[]{:S(2)}) collective-permute-start(bf16[272,256]{1,0:T(8,128)(2,1)S(1)} %pad_maximum_fusion.4.refs_0_), channel_id=1, source_target_pairs={{0,2},{2,0},{16,18},{18,16},{1,3},{3,1},{17,19},{19,17},{4,6},{6,4... | collective-permute-start | bytes 417800 | tf_op jit(solution)/shard_map/ppermute | solution.py:35
  21.9 14.2 %collective-permute-start = (bf16[272,256]{1,0:T(8,128)(2,1)S(1)}, bf16[272,256]{1,0:T(8,128)(2,1)}, u32[]{:S(2)}, u32[]{:S(2)}) collective-permute-start(bf16[272,256]{1,0:T(8,128)(2,1)S(1)} %pad_maximum_fusion.4.refs_0_), channel_id=1, source_target_pairs={{0,16},{2,18},{16,0},{18,2},{1,17},{3,19},{17,1},{19,3},{4,20},{6,... | collective-permute-start | bytes 417800 | tf_op jit(solution)/shard_map/ppermute | solution.py:35
  23.4 34.7 %collective-permute-start.16 = (bf16[512,512]{1,0:T(8,128)(2,1)S(1)}, bf16[512,512]{1,0:T(8,128)(2,1)}, u32[]{:S(2)}, u32[]{:S(2)}) collective-permute-start(bf16[512,512]{1,0:T(8,128)(2,1)S(1)} %copy-done.2), channel_id=1, source_target_pairs={{0,1},{1,0},{2,3},{3,2},{4,5},{5,4},{6,7},{7,6},{8,9},{9,8},{10,11... | collective-permute-start | bytes 1572872 | tf_op jit(solution)/shard_map/ppermute | solution.py:35
  27.0 15.2 %collective-permute-start.2 = (bf16[1040,256]{1,0:T(8,128)(2,1)}, bf16[1040,256]{1,0:T(8,128)(2,1)S(1)}, u32[]{:S(2)}, u32[]{:S(2)}) collective-permute-start(bf16[1040,256]{1,0:T(8,128)(2,1)} %pad_maximum_fusion), channel_id=1, source_target_pairs={{0,18},{2,16},{16,2},{18,0},{1,19},{3,17},{17,3},{19,1},{4,22},{6,... | collective-permute-start | bytes 1597448 | tf_op jit(solution)/shard_map/ppermute | solution.py:35
  36.1 7.0 %collective-permute-start.4 = (bf16[272,256]{1,0:T(8,128)(2,1)}, bf16[272,256]{1,0:T(8,128)(2,1)S(1)}, u32[]{:S(2)}, u32[]{:S(2)}) collective-permute-start(bf16[272,256]{1,0:T(8,128)(2,1)} %collective-permute-done.refs_1_), channel_id=1, source_target_pairs={{0,1},{1,0},{2,3},{3,2},{4,5},{5,4},{6,7},{7,6},{8,9},{9,8},{10,11... | collective-permute-start | bytes 417800 | tf_op jit(solution)/shard_map/ppermute | solution.py:35
  52.5 9.1 %collective-permute-start.19 = (bf16[256,256]{1,0:T(8,128)(2,1)S(1)}, bf16[256,256]{1,0:T(8,128)(2,1)S(1)}, u32[]{:S(2)}, u32[]{:S(2)}) collective-permute-start(bf16[256,256]{1,0:T(8,128)(2,1)S(1)} %copy-done.16), channel_id=1, source_target_pairs={{0,18},{2,16},{16,2},{18,0},{1,19},{3,17},{17,3},{19,1},{4,22},{6,... | collective-permute-start | bytes 393224 | tf_op jit(solution)/shard_map/ppermute | solution.py:35
  52.9 9.5 %collective-permute-start.18 = (bf16[256,256]{1,0:T(8,128)(2,1)S(1)}, bf16[256,256]{1,0:T(8,128)(2,1)S(1)}, u32[]{:S(2)}, u32[]{:S(2)}) collective-permute-start(bf16[256,256]{1,0:T(8,128)(2,1)S(1)} %copy-done.16), channel_id=1, source_target_pairs={{0,2},{2,0},{16,18},{18,16},{1,3},{3,1},{17,19},{19,17},{4,6},{6,4... | collective-permute-start | bytes 393224 | tf_op jit(solution)/shard_map/ppermute | solution.py:35
  54.5 9.0 %collective-permute-start.17 = (bf16[256,256]{1,0:T(8,128)(2,1)S(1)}, bf16[256,256]{1,0:T(8,128)(2,1)S(1)}, u32[]{:S(2)}, u32[]{:S(2)}) collective-permute-start(bf16[256,256]{1,0:T(8,128)(2,1)S(1)} %copy-done.16), channel_id=1, source_target_pairs={{0,16},{2,18},{16,0},{18,2},{1,17},{3,19},{17,1},{19,3},{4,20},{6,... | collective-permute-start | bytes 393224 | tf_op jit(solution)/shard_map/ppermute | solution.py:35
  86.3 7.1 %collective-permute-start.26 = (bf16[4,256,256]{2,1,0:T(8,128)(2,1)}, bf16[4,256,256]{2,1,0:T(8,128)(2,1)S(1)}, u32[]{:S(2)}, u32[]{:S(2)}) collective-permute-start(bf16[4,256,256]{2,1,0:T(8,128)(2,1)} %get-tuple-element.111), channel_id=1, source_target_pairs={{0,1},{1,0},{2,3},{3,2},{4,5},{5,4},{6,7},{7,6},{8,9},{9,8},{10,11... | collective-permute-start | bytes 1572872 | tf_op jit(solution)/shard_map/ppermute | solution.py:35
  97.4 8.4 %collective-permute-start.28 = (bf16[256,256]{1,0:T(8,128)(2,1)S(1)}, bf16[256,256]{1,0:T(8,128)(2,1)S(1)}, u32[]{:S(2)}, u32[]{:S(2)}) collective-permute-start(bf16[256,256]{1,0:T(8,128)(2,1)S(1)} %copy-done.51), channel_id=1, source_target_pairs={{0,2},{2,0},{16,18},{18,16},{1,3},{3,1},{17,19},{19,17},{4,6},{6,4... | collective-permute-start | bytes 393224 | tf_op jit(solution)/shard_map/ppermute | solution.py:35
  99.5 8.8 %collective-permute-start.29 = (bf16[256,256]{1,0:T(8,128)(2,1)S(1)}, bf16[256,256]{1,0:T(8,128)(2,1)S(1)}, u32[]{:S(2)}, u32[]{:S(2)}) collective-permute-start(bf16[256,256]{1,0:T(8,128)(2,1)S(1)} %copy-done.50), channel_id=1, source_target_pairs={{0,18},{2,16},{16,2},{18,0},{1,19},{3,17},{17,3},{19,1},{4,22},{6,... | collective-permute-start | bytes 393224 | tf_op jit(solution)/shard_map/ppermute | solution.py:35
  110.2 7.4 %collective-permute-start.31 = (bf16[256,256]{1,0:T(8,128)(2,1)S(1)}, bf16[256,256]{1,0:T(8,128)(2,1)S(1)}, u32[]{:S(2)}, u32[]{:S(2)}) collective-permute-start(bf16[256,256]{1,0:T(8,128)(2,1)S(1)} %add_convert_fusion.refs_0_), channel_id=1, source_target_pairs={{0,2},{2,0},{16,18},{18,16},{1,3},{3,1},{17,19},{19,17},{4,6},{6,4... | collective-permute-start | bytes 393224 | tf_op jit(solution)/shard_map/ppermute | solution.py:35
  110.2 8.9 %collective-permute-start.30 = (bf16[256,256]{1,0:T(8,128)(2,1)S(1)}, bf16[256,256]{1,0:T(8,128)(2,1)S(1)}, u32[]{:S(2)}, u32[]{:S(2)}) collective-permute-start(bf16[256,256]{1,0:T(8,128)(2,1)S(1)} %add_convert_fusion.refs_0_), channel_id=1, source_target_pairs={{0,16},{2,18},{16,0},{18,2},{1,17},{3,19},{17,1},{19,3},{4,20},{6,... | collective-permute-start | bytes 393224 | tf_op jit(solution)/shard_map/ppermute | solution.py:35
  111.7 7.4 %collective-permute-start.33 = (bf16[256,256]{1,0:T(8,128)(2,1)S(1)}, bf16[256,256]{1,0:T(8,128)(2,1)S(1)}, u32[]{:S(2)}, u32[]{:S(2)}) collective-permute-start(bf16[256,256]{1,0:T(8,128)(2,1)S(1)} %add_convert_fusion.refs_0_), channel_id=1, source_target_pairs={{0,1},{1,0},{2,3},{3,2},{4,5},{5,4},{6,7},{7,6},{8,9},{9,8},{10,11... | collective-permute-start | bytes 393224 | tf_op jit(solution)/shard_map/ppermute | solution.py:35
  126.6 11.1 %collective-permute-start.37 = (f32[2,16,128]{2,1,0:T(8,128)}, f32[2,16,128]{2,1,0:T(8,128)S(1)}, u32[]{:S(2)}, u32[]{:S(2)}) collective-permute-start(f32[2,16,128]{2,1,0:T(8,128)} %get-tuple-element.133), channel_id=1, source_target_pairs={{0,12},{4,0},{8,4},{12,8},{1,13},{5,1},{9,5},{13,9},{2,14},{6,2},{... | collective-permute-start | bytes 49160 | tf_op jit(solution)/shard_map/ppermute | solution.py:35
  146.2 33.8 %all-to-all-start = ((bf16[16,5,64,128]{3,2,1,0:T(8,128)(2,1)}), bf16[16,5,64,128]{3,2,1,0:T(8,128)(2,1)}, u32[]{:S(2)}, u32[]{:S(2)}) async-start(bf16[16,5,64,128]{3,2,1,0:T(8,128)(2,1)} %shard_map.177), calls=%async_computation | async-start | bytes 2621440 | tf_op jit(solution)/shard_map/all_to_all | solution.py:686
  159.3 8.0 %collective-permute-start.41 = (bf16[528,256]{1,0:T(8,128)(2,1)}, bf16[528,256]{1,0:T(8,128)(2,1)S(1)}, u32[]{:S(2)}, u32[]{:S(2)}) collective-permute-start(bf16[528,256]{1,0:T(8,128)(2,1)} %get-tuple-element.152), channel_id=1, source_target_pairs={{0,16},{2,18},{16,0},{18,2},{1,17},{3,19},{17,1},{19,3},{4,20},{6,... | collective-permute-start | bytes 811016 | tf_op jit(solution)/shard_map/ppermute | solution.py:35
  159.3 15.1 %collective-permute-start.42 = (bf16[528,256]{1,0:T(8,128)(2,1)}, bf16[528,256]{1,0:T(8,128)(2,1)S(1)}, u32[]{:S(2)}, u32[]{:S(2)}) collective-permute-start(bf16[528,256]{1,0:T(8,128)(2,1)} %get-tuple-element.153), channel_id=1, source_target_pairs={{0,2},{2,0},{16,18},{18,16},{1,3},{3,1},{17,19},{19,17},{4,6},{6,4... | collective-permute-start | bytes 811016 | tf_op jit(solution)/shard_map/ppermute | solution.py:35
  162.1 14.3 %collective-permute-start.43 = (bf16[528,256]{1,0:T(8,128)(2,1)}, bf16[528,256]{1,0:T(8,128)(2,1)S(1)}, u32[]{:S(2)}, u32[]{:S(2)}) collective-permute-start(bf16[528,256]{1,0:T(8,128)(2,1)} %get-tuple-element.154), channel_id=1, source_target_pairs={{0,18},{2,16},{16,2},{18,0},{1,19},{3,17},{17,3},{19,1},{4,22},{6,... | collective-permute-start | bytes 811016 | tf_op jit(solution)/shard_map/ppermute | solution.py:35
  182.3 14.0 %collective-permute-start.44 = (bf16[384,128]{1,0:T(8,128)(2,1)}, bf16[384,128]{1,0:T(8,128)(2,1)S(1)}, u32[]{:S(2)}, u32[]{:S(2)}) collective-permute-start(bf16[384,128]{1,0:T(8,128)(2,1)} %get-tuple-element.162), channel_id=1, source_target_pairs={{0,0},{2,64},{4,4},{6,68},{8,8},{10,72},{12,12},{14,76},{16,32},{1... | collective-permute-start | bytes 294920 | tf_op jit(solution)/shard_map/ppermute | solution.py:35
  (83 other events, 395.9 us)
Sparse Core Ops, SparseCore 0:
  19.8 49.6 all-gather.2
  96.6 83.4 reduce-scatter.1

commit v2 on v1

--- a/solution.py
+++ b/solution.py
@@ -41,6 +41,11 @@
 
 def swap_core(value):
     return moved(value, ("col",), lambda col: (1 - col,))
+
+
+def by_core(col, near, far):
+    first = col == 0
+    return jnp.where(first, near, far), jnp.where(first, far, near)
 
 
 def dot(a, b, dims):
@@ -367,13 +372,14 @@
             for h in (0, 1):
                 for k in range(3):
                     first = source_row(m, h)
-                    late[m, 2 * r + h, 16 * k : 16 * k + 16] = total[first : first + 16, 128 * k : 128 * k + 128]
-                late[m, 2 * r + h, 48:64] = small[r]
+                    at = 48 * (2 * r + h) + 16 * k
+                    late[m, at : at + 16] = total[first : first + 16, 128 * k : 128 * k + 128]
+            late[m, 256 + 16 * r : 272 + 16 * r] = small[r]
     total = mm(y[...].T, do[...]).astype(low)
     for r in (0, 1):
         for i in range(8):
             for t in range(4):
-                late[8 * r + i, 4, 16 * t : 16 * t + 16] = total[
+                late[8 * r + i, 192 + 16 * t : 208 + 16 * t] = total[
                     16 * i : 16 * i + 16, 512 * r + 128 * t : 512 * r + 128 * t + 128
                 ]
 
@@ -413,24 +419,24 @@
 def deal(place, late, early, settled, *messages):
     row, xl = place[0], place[1]
 
-    def total(block, here):
-        parts = [late[m, block, here].astype(f32) for m in range(16)]
+    def total(here):
+        parts = [late[m, here].astype(f32) for m in range(16)]
         while len(parts) > 1:
             parts = [a + b for a, b in zip(parts[::2], parts[1::2])]
         return parts[0].astype(low)
 
     for j, message in enumerate(messages):
         r, half = row ^ (j >> 1), xl ^ (j & 1)
-        message[0:64] = total(2 * r + half, slice(None))
+        message[0:48] = total(pl.ds(pl.multiple_of(48 * (2 * r + half), 16), 48))
+        message[48:64] = total(rows(16 + r, 16))
         for i in range(10):
             message[64 + 16 * i : 80 + 16 * i] = early[pl.ds(pl.multiple_of((10 * r + i) * 32 + 16 * half, 16), 16)]
-    settled[0:64] = total(4, slice(None))
+    settled[0:64] = total(slice(192, 256))
     settled[64:384] = early[640:960]
 
 
-def place_out(place, settled, m0, m1, m2, m3, g_in, g_out, g_gu, g_down, small, cross):
-    row, xl, col = place[0], place[1], place[2]
-    spot = 2 * row + xl
+def place_out(place, settled, m0, m1, m2, m3, g_in, g_out, g_gu, g_down):
+    spot = 2 * place[0] + place[1]
     got = (m0, m1, m2, m3)
 
     def sender(q, here):
@@ -440,12 +446,10 @@
             jnp.where(spot == (q ^ 1), got[1][here], jnp.where(spot == (q ^ 2), got[2][here], got[3][here])),
         ).astype(f32)
 
-    extra = jnp.zeros((16, 128), f32)
     for q in range(4):
         whole = sender(q, slice(None))
         for k in range(3):
             g_in[k, :, 128 * q : 128 * q + 128] = whole[16 * k : 16 * k + 16]
-        extra += whole[48:64]
         first = 9 * q // 2
         for k in (0, 1):
             for t in range(5):
@@ -455,9 +459,6 @@
                     g_gu[:, k, here] += whole[at : at + 16]
                 else:
                     g_gu[:, k, here] = whole[at : at + 16]
-    swap = col == 1
-    small[...] = jnp.concatenate([jnp.where(swap, extra[2:4], extra[0:2]), extra[4:]], axis=0)
-    cross[...] = jnp.concatenate([jnp.where(swap, extra[0:2], extra[2:4]), extra[:6]], axis=0)
     for t in range(4):
         here = slice(128 * t, 128 * t + 128)
         g_out[:, here] = settled[16 * t : 16 * t + 16].astype(f32)
@@ -681,7 +682,7 @@
         got_ffn,
         total,
     )
-    (late,) = call(mix_weights, [shaped(16, 5, 64, 128, kind=low)], [], place, n_one, dproj, y, do, small)
+    (late,) = call(mix_weights, [shaped(16, 288, 128, kind=low)], [], place, n_one, dproj, y, do, small)
     ringed = [ring(v, k) for k, v in zip((1, 2, 3), parts)]
     late = lax.all_to_all(late, ("y", "z"), 0, 0)
     h_own = lax.dynamic_slice_in_dim(hidden[:256], (2 * row + col) * 256, 256, 1)
@@ -698,23 +699,19 @@
         settled, ("y", "xl", "z", "row"), lambda y, xl, z, r: (2 * r + xl, y % 2, z, y // 2)
     )
     messages = [messages[0]] + [ring(messages[k], k) for k in (1, 2, 3)]
-    grad_in, grad_out, grad_gate_up, grad_down, small, cross = call(
+    extra = sum(message[48:64].astype(f32) for message in messages)
+    mine, cross = by_core(col, extra[0:2], extra[2:4])
+    cross, settled = lax.optimization_barrier((cross, settled))
+    cross = swap_core(cross)
+    grad_in, grad_out, grad_gate_up, grad_down = call(
         place_out,
-        [
-            shaped(3, 16, 512),
-            shaped(16, 512),
-            shaped(16, 2, 2304),
-            shaped(72, 512),
-            shaped(14, 128),
-            shaped(8, 128),
-        ],
+        [shaped(3, 16, 512), shaped(16, 512), shaped(16, 2, 2304), shaped(72, 512)],
         [],
         place,
         settled,
         *messages,
     )
-    cross = swap_core(cross)
-    small = jnp.concatenate([small[:2] + cross[:2], small[2:10]]).reshape(5, 256)
+    small = jnp.concatenate([mine + cross, extra[4:12]]).reshape(5, 256)
     small = cut(small, 8 * yy + 4 * xl + zz, 8, 1)
     return (
         mixed,

time: 212 us -> 210 us (level)
  the two profiles are of different devices: /device:TPU:1 before, /device:TPU:38 now
where the time goes in v2:
time: 210 us; the launch traced here: 207 us
  Pallas kernels  57.7 us (27%)
  starting transfers between devices  57.1 us (27%)
  waiting for transfers between devices  50 us (24%)
  local copies, waits for them, and re-layouts  24.1 us (11%)
  between operations  14.9 us (7%)
  other arithmetic  3.02 us (1%)
    pallas_call x13, Pallas kernels, call(): pl.pallas_call(body, out_shape=outs, in_specs=[pl.BlockSpec(memory_space=...  57.7 us
    ppermute x49, waiting for transfers between devices, moved(): return lax.ppermute(value, axes if len(axes) > 1 else axes[0], pairs)  49.9 us
    ppermute x49, starting transfers between devices, moved(): return lax.ppermute(value, axes if len(axes) > 1 else axes[0], pairs)  45.5 us
    all_to_all x1, starting transfers between devices, local(): late = lax.all_to_all(late, ('y', 'z'), 0, 0)  11.6 us
    unnamed x101, local copies, waits for them, and re-layouts  10.2 us
  transfers between devices with their start and end apart: 52, of which 23 were waited for; matrix products, arithmetic and copies ran while one was open for 8% of the time, Pallas kernels for 19%

profile of v2, /device:TPU:38, one launch (start us, length us, event | category | flops | bytes accessed | tf_op | source)
XLA Modules:
  0.0 206.8 jit_solution(14490414692775800988)
XLA Ops:
  12.6 4.3 %collective-permute-done.25 = bf16[128,128]{1,0:T(8,128)(2,1)S(1)} collective-permute-done((bf16[128,128]{1,0:T(8,128)(2,1)S(1)}, bf16[128,128]{1,0:T(8,128)(2,1)S(1)}, u32[]{:S(2)}, u32[]{:S(2)}) %collective-permute-start.25) | collective-permute-done | bytes 32800 | tf_op jit(solution)/shard_map/ppermute | solution.py:35
  26.7 3.3 %constant_dynamic-slice_fusion.8 = bf16[512,2,640]{2,1,0:T(2,128)(2,1)} fusion(bf16[512,2,2304]{2,1,0:T(2,128)(2,1)} %param.17, s32[]{:T(128)S(6)} %select_n.57), kind=kLoop, calls=%fused_computation.19 | loop fusion | bytes 2621444 | tf_op jit(solution)/shard_map/dynamic-slice.1
  35.3 4.1 %collective-permute-done.2.refs_3_ = bf16[1040,256]{1,0:T(8,128)(2,1)S(1)} collective-permute-done((bf16[1040,256]{1,0:T(8,128)(2,1)}, bf16[1040,256]{1,0:T(8,128)(2,1)S(1)}, u32[]{:S(2)}, u32[]{:S(2)}) %collective-permute-start.2) | collective-permute-done | bytes 532512 | tf_op jit(solution)/shard_map/ppermute | solution.py:35
  41.5 4.7 %shard_map.169 = (bf16[512,1024]{1,0:T(8,128)(2,1)}, bf16[512,1024]{1,0:T(8,128)(2,1)}, f32[16,1024]{1,0:T(8,128)}, f32[512,128]{1,0:T(8,128)}, f32[512,128]{1,0...) custom-call(s32[5]{0:T(128)} %stack.55.place, ...), custom_call_target="tpu_custom_call" | custom-call | tf_op jit(solution)/shard_map/pallas_call | solution.py:77
  63.7 3.4 %collective-permute-done.10.refs_2_ = bf16[512,128]{1,0:T(8,128)(2,1)S(1)} collective-permute-done((bf16[512,128]{1,0:T(8,128)(2,1)}, bf16[512,128]{1,0:T(8,128)(2,1)S(1)}, u32[]{:S(2)}, u32[]{:S(2)}) %collective-permute-start.10) | collective-permute-done | bytes 131104 | tf_op jit(solution)/shard_map/ppermute | solution.py:35
  69.2 14.4 %shard_map.171 = (f32[512,1024]{1,0:T(8,128)}, bf16[512,1024]{1,0:T(8,128)(2,1)}, bf16[512,640]{1,0:T(8,128)(2,1)}, bf16[512,640]{1,0:T(8,128)(2,1)}, bf16[512,6...) custom-call(s32[5]{0:T(128)} %stack.55.place, ...), custom_call_target="tpu_custom_call" | custom-call | tf_op jit(solution)/shard_map/pallas_call | solution.py:77
  83.9 6.7 %shard_map.173 = bf16[16,960,128]{2,1,0:T(8,128)(2,1)} custom-call(s32[5]{0:T(128)} %stack.55.place, bf16[512,1024]{1,0:T(8,128)(2,1)} %get-tuple-element.113.n, bf16[512,640]{1,0:T(8,128)(2,1)} %get-tuple-element.128.act, bf16[512,640]{1,0:T(8,128)(2,1)} %get-tuple-element.115.dgate, bf16[512,640]{1,0:T(8,128)(2,1)} %get-tuple-element.116.dup, ...), custom_call_target="tpu_custom_call" | custom-call | tf_op jit(solution)/shard_map/pallas_call | solution.py:77
  95.1 2.8 %collective-permute-start.28 = (bf16[256,256]{1,0:T(8,128)(2,1)S(1)}, bf16[256,256]{1,0:T(8,128)(2,1)S(1)}, u32[]{:S(2)}, u32[]{:S(2)}) collective-permute-start(bf16[256,256]{1,0:T(8,128)(2,1)S(1)} %copy-done.47), channel_id=1, source_target_pairs={{0,2},{2,0},{16,18},{18,16},{1,3},{3,1},{17,19},{19,17},{4,6},{6,4... | collective-permute-start | bytes 393224 | tf_op jit(solution)/shard_map/ppermute | solution.py:35
  100.8 3.7 %collective-permute-done.28 = bf16[256,256]{1,0:T(8,128)(2,1)S(1)} collective-permute-done((bf16[256,256]{1,0:T(8,128)(2,1)S(1)}, bf16[256,256]{1,0:T(8,128)(2,1)S(1)}, u32[]{:S(2)}, u32[]{:S(2)}) %collective-permute-start.28) | collective-permute-done | bytes 131104 | tf_op jit(solution)/shard_map/ppermute | solution.py:35
  108.3 2.8 %collective-permute-start.30 = (bf16[256,256]{1,0:T(8,128)(2,1)S(1)}, bf16[256,256]{1,0:T(8,128)(2,1)S(1)}, u32[]{:S(2)}, u32[]{:S(2)}) collective-permute-start(bf16[256,256]{1,0:T(8,128)(2,1)S(1)} %add_convert_fusion.refs_0_), channel_id=1, source_target_pairs={{0,16},{2,18},{16,0},{18,2},{1,17},{3,19},{17,1},{19,3},{4,20},{6,... | collective-permute-start | bytes 393224 | tf_op jit(solution)/shard_map/ppermute | solution.py:35
  111.1 4.9 %collective-permute-done.32.refs_3_ = bf16[256,256]{1,0:T(8,128)(2,1)S(1)} collective-permute-done((bf16[256,256]{1,0:T(8,128)(2,1)S(1)}, bf16[256,256]{1,0:T(8,128)(2,1)S(1)}, u32[]{:S(2)}, u32[]{:S(2)}) %collective-permute-start.32) | collective-permute-done | bytes 131104 | tf_op jit(solution)/shard_map/ppermute | solution.py:35
  118.7 5.7 %shard_map.174 = (f32[256,256]{1,0:T(8,128)}, bf16[512,1024]{1,0:T(8,128)(2,1)}, f32[512,128]{1,0:T(8,128)}, f32[512,128]{1,0:T(8,128)}, f32[2,16,128]{2,1,0:T(8...) custom-call(s32[5]{0:T(128)} %stack.55.place, bf16[256,256]{1,0:T(8,128)(2,1)} %copy-done.7, bf16[256,256]{1,0:T(8,128)(2,1)} %copy-done.30, ...), custom_call_target="tpu_custom_call" | custom-call | tf_op jit(solution)/shard_map/pallas_call | solution.py:77
  126.5 3.7 %shard_map.175 = (f32[4,256,256]{2,1,0:T(8,128)}, bf16[4,256,256]{2,1,0:T(8,128)(2,1)}) custom-call(s32[5]{0:T(128)} %stack.55.place, bf16[512,640]{1,0:T(8,128)(2,1)} %get-tuple-element.128.act, bf16[640,512]{1,0:T(8,128)(2,1)} %constant_dynamic-slice_fusion.7.refs_13_.down_own, bf16[640,512]{1,0:T(8,128)(2,1)} %get-tuple-element.129.down_far), custom_call_target="tpu_custom_call" | custom-call | tf_op jit(solution)/shard_map/pallas_call | solution.py:77
  130.8 4.3 %shard_map.176 = (bf16[512,384]{1,0:T(8,128)(2,1)}, f32[4,256,256]{2,1,0:T(8,128)}, bf16[4,272,256]{2,1,0:T(8,128)(2,1)}, f32[2,8,256]{2,1,0:T(8,128)}, bf16[2,16,128]{2,1,0:T(8,128)(2,1)}) custom-call(s32[5]{0:T(128)} %stack.55.place, f32[512,128]{1,0:T(8,128)} %get-tuple-element.131.refs_0_, f32[512,128]{1,0:T(8,128)} %get-tuple-element.132.refs_1_, ...), custom_call_target="tpu_custom_call" | custom-call | tf_op jit(solution)/shard_map/pallas_call | solution.py:77
  135.2 3.7 %shard_map.177 = bf16[16,288,128]{2,1,0:T(8,128)(2,1)} custom-call(s32[5]{0:T(128)} %stack.55.place, bf16[512,1024]{1,0:T(8,128)(2,1)} %get-tuple-element.94.n, bf16[512,384]{1,0:T(8,128)(2,1)} %get-tuple-element.141.dproj, bf16[512,128]{1,0:T(8,128)(2,1)} %get-tuple-element.103.refs_0_.y, bf16[512,1024]{1,0:T(8,128)(2,1)} %get-tuple-element.142.do, ...), custom_call_target="tpu_custom_call" | custom-call | tf_op jit(solution)/shard_map/pallas_call | solution.py:77
  138.8 11.6 %all-to-all-start = ((bf16[16,288,128]{2,1,0:T(8,128)(2,1)}), bf16[16,288,128]{2,1,0:T(8,128)(2,1)S(1)}, u32[]{:S(2)}, u32[]{:S(2)}) async-start(bf16[16,288,128]{2,1,0:T(8,128)(2,1)} %shard_map.177), calls=%async_computation | async-start | bytes 2359296 | tf_op jit(solution)/shard_map/all_to_all | solution.py:687
  154.3 3.0 %shard_map.178 = (f32[256,256]{1,0:T(8,128)}, f32[256,256]{1,0:T(8,128)}, f32[8,256]{1,0:T(8,128)}, bf16[528,256]{1,0:T(8,128)(2,1)}, bf16[528,256]{1,0:T(8,128)(2,1)}, /*index=5*/bf16[528,256]{1,0:T(8,128)(2,1)}) custom-call(s32[5]{0:T(128)} %stack.55.place, f32[4,256,256]{2,1,0:T(8,128)} %get-tuple-element.144.keep, bf16[4,272,256]{2,1,0:T(8,128)(2,1)} %copy-done.5, ...), custom_call_target="tpu_custom_call" | custom-call | tf_op jit(solution)/shard_map/pallas_call | solution.py:77
  157.3 2.7 %collective-permute-start.42 = (bf16[528,256]{1,0:T(8,128)(2,1)}, bf16[528,256]{1,0:T(8,128)(2,1)}, u32[]{:S(2)}, u32[]{:S(2)}) collective-permute-start(bf16[528,256]{1,0:T(8,128)(2,1)} %get-tuple-element.153), channel_id=1, source_target_pairs={{0,2},{2,0},{16,18},{18,16},{1,3},{3,1},{17,19},{19,17},{4,6},{6,4... | collective-permute-start | bytes 811016 | tf_op jit(solution)/shard_map/ppermute | solution.py:35
  164.1 2.9 %collective-permute-done.41.got1 = bf16[528,256]{1,0:T(8,128)(2,1)} collective-permute-done((bf16[528,256]{1,0:T(8,128)(2,1)}, bf16[528,256]{1,0:T(8,128)(2,1)}, u32[]{:S(2)}, u32[]{:S(2)}) %collective-permute-start.41) | collective-permute-done | bytes 270368 | tf_op jit(solution)/shard_map/ppermute | solution.py:35
  166.9 5.8 %collective-permute-done.42.got2 = bf16[528,256]{1,0:T(8,128)(2,1)} collective-permute-done((bf16[528,256]{1,0:T(8,128)(2,1)}, bf16[528,256]{1,0:T(8,128)(2,1)}, u32[]{:S(2)}, u32[]{:S(2)}) %collective-permute-start.42) | collective-permute-done | bytes 270368 | tf_op jit(solution)/shard_map/ppermute | solution.py:35
  175.3 2.9 %shard_map.179 = (bf16[256,256]{1,0:T(8,128)(2,1)}, bf16[256,256]{1,0:T(8,128)(2,1)}) custom-call(s32[5]{0:T(128)} %stack.55.place, f32[256,256]{1,0:T(8,128)} %get-tuple-element.149.own, f32[256,256]{1,0:T(8,128)} %get-tuple-element.150.own_ffn, f32[8,256]{1,0:T(8,128)} %get-tuple-element.151.mass, bf16[528,256]{1,0:T(8,128)(2,1)} %collective-permute-done.41.got1, ...), custom_call_target="tpu_custom_call" | custom-call | tf_op jit(solution)/shard_map/pallas_call | solution.py:77
  181.3 3.4 %collective-permute-start.45 = (bf16[224,128]{1,0:T(8,128)(2,1)}, bf16[224,128]{1,0:T(8,128)(2,1)S(1)}, u32[]{:S(2)}, u32[]{:S(2)}) collective-permute-start(bf16[224,128]{1,0:T(8,128)(2,1)} %get-tuple-element.164), channel_id=1, source_target_pairs={{0,2},{2,0},{16,18},{18,16},{1,3},{3,1},{17,19},{19,17},{4,6},{6,4... | collective-permute-start | bytes 172040 | tf_op jit(solution)/shard_map/ppermute | solution.py:35
  186.0 5.9 %collective-permute-start.47 = (bf16[384,128]{1,0:T(8,128)(2,1)}, bf16[384,128]{1,0:T(8,128)(2,1)S(1)}, u32[]{:S(2)}, u32[]{:S(2)}) collective-permute-start(bf16[384,128]{1,0:T(8,128)(2,1)} %get-tuple-element.166), channel_id=1, source_target_pairs={{0,0},{2,64},{4,4},{6,68},{8,8},{10,72},{12,12},{14,76},{16,32},{1... | collective-permute-start | bytes 294920 | tf_op jit(solution)/shard_map/ppermute | solution.py:35
  192.7 3.3 %collective-permute-done.47.settled = bf16[384,128]{1,0:T(8,128)(2,1)S(1)} collective-permute-done((bf16[384,128]{1,0:T(8,128)(2,1)}, bf16[384,128]{1,0:T(8,128)(2,1)S(1)}, u32[]{:S(2)}, u32[]{:S(2)}) %collective-permute-start.47) | collective-permute-done | bytes 98336 | tf_op jit(solution)/shard_map/ppermute | solution.py:35
  (248 shorter events, 77.9 us)
Async XLA Ops:
  7.2 61.9 %all-gather.3.cloned.1.call-start = ((), (), s32[]{:S(2)}) async-start(), calls=%async_computation.3 | async-start | bytes 3342336 | tf_op jit(solution)/shard_map/all_gather | solution.py:516
  18.5 159.7 %reduce-scatter.2.cloned.1.call-start = ((), (), s32[]{:S(2)}) async-start(), calls=%async_computation.2 | async-start | bytes 4177920 | tf_op jit(solution)/shard_map/reduce_scatter | solution.py:619
  18.8 20.7 %collective-permute-start.3 = (bf16[272,256]{1,0:T(8,128)(2,1)S(1)}, bf16[272,256]{1,0:T(8,128)(2,1)}, u32[]{:S(2)}, u32[]{:S(2)}) collective-permute-start(bf16[272,256]{1,0:T(8,128)(2,1)S(1)} %pad_maximum_fusion.4.refs_0_), channel_id=1, source_target_pairs={{0,1},{1,0},{2,3},{3,2},{4,5},{5,4},{6,7},{7,6},{8,9},{9,8},{10,11... | collective-permute-start | bytes 417800 | tf_op jit(solution)/shard_map/ppermute | solution.py:35
  19.0 16.0 %collective-permute-start.1 = (bf16[272,256]{1,0:T(8,128)(2,1)S(1)}, bf16[272,256]{1,0:T(8,128)(2,1)}, u32[]{:S(2)}, u32[]{:S(2)}) collective-permute-start(bf16[272,256]{1,0:T(8,128)(2,1)S(1)} %pad_maximum_fusion.4.refs_0_), channel_id=1, source_target_pairs={{0,2},{2,0},{16,18},{18,16},{1,3},{3,1},{17,19},{19,17},{4,6},{6,4... | collective-permute-start | bytes 417800 | tf_op jit(solution)/shard_map/ppermute | solution.py:35
  19.2 15.6 %collective-permute-start = (bf16[272,256]{1,0:T(8,128)(2,1)S(1)}, bf16[272,256]{1,0:T(8,128)(2,1)}, u32[]{:S(2)}, u32[]{:S(2)}) collective-permute-start(bf16[272,256]{1,0:T(8,128)(2,1)S(1)} %pad_maximum_fusion.4.refs_0_), channel_id=1, source_target_pairs={{0,16},{2,18},{16,0},{18,2},{1,17},{3,19},{17,1},{19,3},{4,20},{6,... | collective-permute-start | bytes 417800 | tf_op jit(solution)/shard_map/ppermute | solution.py:35
  20.5 34.8 %collective-permute-start.16 = (bf16[512,512]{1,0:T(8,128)(2,1)S(1)}, bf16[512,512]{1,0:T(8,128)(2,1)}, u32[]{:S(2)}, u32[]{:S(2)}) collective-permute-start(bf16[512,512]{1,0:T(8,128)(2,1)S(1)} %copy-done.3), channel_id=1, source_target_pairs={{0,1},{1,0},{2,3},{3,2},{4,5},{5,4},{6,7},{7,6},{8,9},{9,8},{10,11... | collective-permute-start | bytes 1572872 | tf_op jit(solution)/shard_map/ppermute | solution.py:35
  23.4 15.9 %collective-permute-start.2 = (bf16[1040,256]{1,0:T(8,128)(2,1)}, bf16[1040,256]{1,0:T(8,128)(2,1)S(1)}, u32[]{:S(2)}, u32[]{:S(2)}) collective-permute-start(bf16[1040,256]{1,0:T(8,128)(2,1)} %pad_maximum_fusion), channel_id=1, source_target_pairs={{0,18},{2,16},{16,2},{18,0},{1,19},{3,17},{17,3},{19,1},{4,22},{6,... | collective-permute-start | bytes 1597448 | tf_op jit(solution)/shard_map/ppermute | solution.py:35
  48.8 9.2 %collective-permute-start.20 = (bf16[256,256]{1,0:T(8,128)(2,1)S(1)}, bf16[256,256]{1,0:T(8,128)(2,1)S(1)}, u32[]{:S(2)}, u32[]{:S(2)}) collective-permute-start(bf16[256,256]{1,0:T(8,128)(2,1)S(1)} %copy-done.14), channel_id=1, source_target_pairs={{0,1},{1,0},{2,3},{3,2},{4,5},{5,4},{6,7},{7,6},{8,9},{9,8},{10,11... | collective-permute-start | bytes 393224 | tf_op jit(solution)/shard_map/ppermute | solution.py:35
  48.9 9.3 %collective-permute-start.19 = (bf16[256,256]{1,0:T(8,128)(2,1)S(1)}, bf16[256,256]{1,0:T(8,128)(2,1)S(1)}, u32[]{:S(2)}, u32[]{:S(2)}) collective-permute-start(bf16[256,256]{1,0:T(8,128)(2,1)S(1)} %copy-done.14), channel_id=1, source_target_pairs={{0,18},{2,16},{16,2},{18,0},{1,19},{3,17},{17,3},{19,1},{4,22},{6,... | collective-permute-start | bytes 393224 | tf_op jit(solution)/shard_map/ppermute | solution.py:35
  51.6 7.9 %collective-permute-start.18 = (bf16[256,256]{1,0:T(8,128)(2,1)S(1)}, bf16[256,256]{1,0:T(8,128)(2,1)S(1)}, u32[]{:S(2)}, u32[]{:S(2)}) collective-permute-start(bf16[256,256]{1,0:T(8,128)(2,1)S(1)} %copy-done.14), channel_id=1, source_target_pairs={{0,2},{2,0},{16,18},{18,16},{1,3},{3,1},{17,19},{19,17},{4,6},{6,4... | collective-permute-start | bytes 393224 | tf_op jit(solution)/shard_map/ppermute | solution.py:35
  51.6 8.7 %collective-permute-start.17 = (bf16[256,256]{1,0:T(8,128)(2,1)S(1)}, bf16[256,256]{1,0:T(8,128)(2,1)S(1)}, u32[]{:S(2)}, u32[]{:S(2)}) collective-permute-start(bf16[256,256]{1,0:T(8,128)(2,1)S(1)} %copy-done.14), channel_id=1, source_target_pairs={{0,16},{2,18},{16,0},{18,2},{1,17},{3,19},{17,1},{19,3},{4,20},{6,... | collective-permute-start | bytes 393224 | tf_op jit(solution)/shard_map/ppermute | solution.py:35
  59.5 7.6 %collective-permute-start.10 = (bf16[512,128]{1,0:T(8,128)(2,1)}, bf16[512,128]{1,0:T(8,128)(2,1)S(1)}, u32[]{:S(2)}, u32[]{:S(2)}) collective-permute-start(bf16[512,128]{1,0:T(8,128)(2,1)} %get-tuple-element.103.refs_0_.y), channel_id=1, source_target_pairs={{0,2},{2,0},{16,18},{18,16},{1,3},{3,1},{17,19},{19,17},{4,6},{6,4... | collective-permute-start | bytes 393224 | tf_op jit(solution)/shard_map/ppermute | solution.py:35
  95.1 9.4 %collective-permute-start.28 = (bf16[256,256]{1,0:T(8,128)(2,1)S(1)}, bf16[256,256]{1,0:T(8,128)(2,1)S(1)}, u32[]{:S(2)}, u32[]{:S(2)}) collective-permute-start(bf16[256,256]{1,0:T(8,128)(2,1)S(1)} %copy-done.47), channel_id=1, source_target_pairs={{0,2},{2,0},{16,18},{18,16},{1,3},{3,1},{17,19},{19,17},{4,6},{6,4... | collective-permute-start | bytes 393224 | tf_op jit(solution)/shard_map/ppermute | solution.py:35
  98.0 8.9 %collective-permute-start.29 = (bf16[256,256]{1,0:T(8,128)(2,1)S(1)}, bf16[256,256]{1,0:T(8,128)(2,1)S(1)}, u32[]{:S(2)}, u32[]{:S(2)}) collective-permute-start(bf16[256,256]{1,0:T(8,128)(2,1)S(1)} %copy-done.46), channel_id=1, source_target_pairs={{0,18},{2,16},{16,2},{18,0},{1,19},{3,17},{17,3},{19,1},{4,22},{6,... | collective-permute-start | bytes 393224 | tf_op jit(solution)/shard_map/ppermute | solution.py:35
  107.0 9.1 %collective-permute-start.32 = (bf16[256,256]{1,0:T(8,128)(2,1)S(1)}, bf16[256,256]{1,0:T(8,128)(2,1)S(1)}, u32[]{:S(2)}, u32[]{:S(2)}) collective-permute-start(bf16[256,256]{1,0:T(8,128)(2,1)S(1)} %add_convert_fusion.refs_0_), channel_id=1, source_target_pairs={{0,18},{2,16},{16,2},{18,0},{1,19},{3,17},{17,3},{19,1},{4,22},{6,... | collective-permute-start | bytes 393224 | tf_op jit(solution)/shard_map/ppermute | solution.py:35
  108.3 7.8 %collective-permute-start.31 = (bf16[256,256]{1,0:T(8,128)(2,1)S(1)}, bf16[256,256]{1,0:T(8,128)(2,1)S(1)}, u32[]{:S(2)}, u32[]{:S(2)}) collective-permute-start(bf16[256,256]{1,0:T(8,128)(2,1)S(1)} %add_convert_fusion.refs_0_), channel_id=1, source_target_pairs={{0,2},{2,0},{16,18},{18,16},{1,3},{3,1},{17,19},{19,17},{4,6},{6,4... | collective-permute-start | bytes 393224 | tf_op jit(solution)/shard_map/ppermute | solution.py:35
  108.3 8.4 %collective-permute-start.30 = (bf16[256,256]{1,0:T(8,128)(2,1)S(1)}, bf16[256,256]{1,0:T(8,128)(2,1)S(1)}, u32[]{:S(2)}, u32[]{:S(2)}) collective-permute-start(bf16[256,256]{1,0:T(8,128)(2,1)S(1)} %add_convert_fusion.refs_0_), channel_id=1, source_target_pairs={{0,16},{2,18},{16,0},{18,2},{1,17},{3,19},{17,1},{19,3},{4,20},{6,... | collective-permute-start | bytes 393224 | tf_op jit(solution)/shard_map/ppermute | solution.py:35
  138.8 39.3 %all-to-all-start = ((bf16[16,288,128]{2,1,0:T(8,128)(2,1)}), bf16[16,288,128]{2,1,0:T(8,128)(2,1)S(1)}, u32[]{:S(2)}, u32[]{:S(2)}) async-start(bf16[16,288,128]{2,1,0:T(8,128)(2,1)} %shard_map.177), calls=%async_computation | async-start | bytes 2359296 | tf_op jit(solution)/shard_map/all_to_all | solution.py:687
  157.3 9.6 %collective-permute-start.41 = (bf16[528,256]{1,0:T(8,128)(2,1)}, bf16[528,256]{1,0:T(8,128)(2,1)}, u32[]{:S(2)}, u32[]{:S(2)}) collective-permute-start(bf16[528,256]{1,0:T(8,128)(2,1)} %get-tuple-element.152), channel_id=1, source_target_pairs={{0,16},{2,18},{16,0},{18,2},{1,17},{3,19},{17,1},{19,3},{4,20},{6,... | collective-permute-start | bytes 811016 | tf_op jit(solution)/shard_map/ppermute | solution.py:35
  157.3 15.4 %collective-permute-start.42 = (bf16[528,256]{1,0:T(8,128)(2,1)}, bf16[528,256]{1,0:T(8,128)(2,1)}, u32[]{:S(2)}, u32[]{:S(2)}) collective-permute-start(bf16[528,256]{1,0:T(8,128)(2,1)} %get-tuple-element.153), channel_id=1, source_target_pairs={{0,2},{2,0},{16,18},{18,16},{1,3},{3,1},{17,19},{19,17},{4,6},{6,4... | collective-permute-start | bytes 811016 | tf_op jit(solution)/shard_map/ppermute | solution.py:35
  160.0 15.3 %collective-permute-start.43 = (bf16[528,256]{1,0:T(8,128)(2,1)}, bf16[528,256]{1,0:T(8,128)(2,1)}, u32[]{:S(2)}, u32[]{:S(2)}) collective-permute-start(bf16[528,256]{1,0:T(8,128)(2,1)} %get-tuple-element.154), channel_id=1, source_target_pairs={{0,18},{2,16},{16,2},{18,0},{1,19},{3,17},{17,3},{19,1},{4,22},{6,... | collective-permute-start | bytes 811016 | tf_op jit(solution)/shard_map/ppermute | solution.py:35
  181.3 10.6 %collective-permute-start.44 = (bf16[224,128]{1,0:T(8,128)(2,1)}, bf16[224,128]{1,0:T(8,128)(2,1)S(1)}, u32[]{:S(2)}, u32[]{:S(2)}) collective-permute-start(bf16[224,128]{1,0:T(8,128)(2,1)} %get-tuple-element.163), channel_id=1, source_target_pairs={{0,16},{2,18},{16,0},{18,2},{1,17},{3,19},{17,1},{19,3},{4,20},{6,... | collective-permute-start | bytes 172040 | tf_op jit(solution)/shard_map/ppermute | solution.py:35
  181.3 10.7 %collective-permute-start.45 = (bf16[224,128]{1,0:T(8,128)(2,1)}, bf16[224,128]{1,0:T(8,128)(2,1)S(1)}, u32[]{:S(2)}, u32[]{:S(2)}) collective-permute-start(bf16[224,128]{1,0:T(8,128)(2,1)} %get-tuple-element.164), channel_id=1, source_target_pairs={{0,2},{2,0},{16,18},{18,16},{1,3},{3,1},{17,19},{19,17},{4,6},{6,4... | collective-permute-start | bytes 172040 | tf_op jit(solution)/shard_map/ppermute | solution.py:35
  186.0 10.0 %collective-permute-start.47 = (bf16[384,128]{1,0:T(8,128)(2,1)}, bf16[384,128]{1,0:T(8,128)(2,1)S(1)}, u32[]{:S(2)}, u32[]{:S(2)}) collective-permute-start(bf16[384,128]{1,0:T(8,128)(2,1)} %get-tuple-element.166), channel_id=1, source_target_pairs={{0,0},{2,64},{4,4},{6,68},{8,8},{10,72},{12,12},{14,76},{16,32},{1... | collective-permute-start | bytes 294920 | tf_op jit(solution)/shard_map/ppermute | solution.py:35
  (79 other events, 346.8 us)
Sparse Core Ops, SparseCore 0:
  18.6 49.0 all-gather.2
  93.8 82.6 reduce-scatter.1

commit v3 on v2

--- a/solution.py
+++ b/solution.py
@@ -72,13 +72,14 @@
     return jax.ShapeDtypeStruct(shape, kind)
 
 
-def call(body, outs, scratch, place, *args):
-    spec = pl.BlockSpec(memory_space=pltpu.VMEM)
+def call(body, outs, scratch, place, *args, loose_in=(), loose_out=()):
+    spec, loose = pl.BlockSpec(memory_space=pltpu.VMEM), pl.BlockSpec(memory_space=pl.ANY)
     return pl.pallas_call(
         body,
         out_shape=outs,
-        in_specs=[pl.BlockSpec(memory_space=pltpu.SMEM)] + [spec] * len(args),
-        out_specs=[spec] * len(outs),
+        in_specs=[pl.BlockSpec(memory_space=pltpu.SMEM)]
+        + [loose if i in loose_in else spec for i in range(len(args))],
+        out_specs=[loose if i in loose_out else spec for i in range(len(outs))],
         scratch_shapes=scratch,
         compiler_params=pltpu.CompilerParams(vmem_limit_bytes=56 * 2**20),
     )(place, *args)
@@ -161,10 +162,20 @@
 
 def feed(place, *refs):
     near, far = refs[0:4], refs[4:8]
-    x, gain, out_own, out_swap, gu_own, down_own = refs[8:14]
+    x_in, gain, out_own, out_swap, gu_in, down_in = refs[8:14]
     df_near, df_far, packs = refs[14:18], refs[18:22], refs[22]
-    hidden, n, act, dgate, dup, keep, send, df, down_far, out_row = refs[23:33]
-    y, wide, gate, up, dact, gu_far, out_far = refs[33:]
+    hidden_out, n_out, act, dgate, dup, keep, send, df_out, down_out, out_row = refs[23:33]
+    y, wide, gate, up, dact, gu_far, out_far, x, gu_own, down_own, hidden, n, df, down_far, sems = refs[33:]
+    ins = [
+        pltpu.make_async_copy(a, b, sems.at[i])
+        for i, (a, b) in enumerate(((x_in, x), (gu_in, gu_own), (down_in, down_own)))
+    ]
+    outs = [
+        pltpu.make_async_copy(a, b, sems.at[3 + i])
+        for i, (a, b) in enumerate(((df, df_out), (down_far, down_out), (hidden, hidden_out), (n, n_out)))
+    ]
+    for copy in ins:
+        copy.start()
     row, xl, col = place[0], place[1], place[2]
     q = 2 * row + xl
     for m in range(16):
@@ -184,9 +195,13 @@
         y[:, lanes(col * 4 + (q ^ k), 128)] = near[k][...]
         y[:, lanes((1 - col) * 4 + (q ^ k), 128)] = far[k][...]
     assemble(df, row, col, df_near, df_far)
+    outs[0].start()
+    outs[1].start()
     y_own, y_far = y[:, lanes(col, 512)], y[:, lanes(1 - col, 512)]
     wide[:, lanes(row, 512)] = mm(y_own, out_own[...]) + mm(y_far, out_swap[...])
     wide[:, lanes(1 - row, 512)] = mm(y_own, out_far[:512]) + mm(y_far, out_far[512:])
+
+    ins[0].wait()
 
     @pl.loop(0, 8)
     def _(i):
@@ -194,9 +209,13 @@
         hidden[rows(i, 64)] = h
         n[rows(i, 64)] = (h * norm_scale(h) * gain[8:9]).astype(low)
 
+    outs[2].start()
+    outs[3].start()
+    ins[1].wait()
     n_own, n_far = n[:, lanes(row, 512)], n[:, lanes(1 - row, 512)]
     gate[...] = mm(n_own, gu_own[0]) + mm(n_far, gu_far[0])
     up[...] = mm(n_own, gu_own[1]) + mm(n_far, gu_far[1])
+    ins[2].wait()
     dact[...] = mm_t(df[:, lanes(row, 512)], down_own[...]) + mm_t(df[:, lanes(1 - row, 512)], down_far[...])
     lane = lax.broadcasted_iota(jnp.int32, (64, 640), 1) - 64 * xl
     mine = (lane >= 0) & (lane < 576)
@@ -216,6 +235,8 @@
     for k, w in ((0, gu_own), (1, gu_far)):
         wide[:, 512 * k : 512 * k + 512] = mm_t(dgate[...], w[0]) + mm_t(dup[...], w[1])
     part(wide, keep, send, col)
+    for copy in outs:
+        copy.wait()
 
 
 def part(wide, keep, send, col):
@@ -235,8 +256,29 @@
     return 128 * (m // 4) + 64 * half + 16 * (m % 4)
 
 
-def feed_weights(place, n, act, dgate, dup, df, early, wide):
+def feed_weights(place, n_in, act, dgate_in, dup_in, df, early_out, wide, early, n, dgate, dup, sems):
     xl = place[1]
+    ins = [
+        pltpu.make_async_copy(a, b, sems.at[i])
+        for i, (a, b) in enumerate(((n_in, n), (dgate_in, dgate), (dup_in, dup)))
+    ]
+    spans = [pl.ds(640, 320)] + [pl.ds((2 * r + k) * 160, 160) for k in (0, 1) for r in (0, 1)]
+    outs = [
+        pltpu.make_async_copy(early.at[:, span], early_out.at[:, span], sems.at[3 + i])
+        for i, span in enumerate(spans)
+    ]
+    for copy in ins:
+        copy.start()
+    wide[...] = mm(act[...].T, df[...])
+    for i in range(8):
+        some = wide[pl.ds(pl.multiple_of(64 * xl + 72 * i, 8), 72)]
+        some = jnp.concatenate([some, jnp.zeros((8, 1024), f32)]).astype(low)
+        for r in (0, 1):
+            for t in range(4):
+                early[8 * r + i, 640 + 80 * t : 720 + 80 * t] = some[:, 512 * r + 128 * t : 512 * r + 128 * t + 128]
+    outs[0].start()
+    for copy in ins:
+        copy.wait()
     n_t = n[...].T
     for k, g in ((0, dgate), (1, dup)):
         for r in (0, 1):
@@ -247,13 +289,9 @@
                         at = ((r * 2 + k) * 5 + t) * 32 + 16 * h
                         first = source_row(m, h)
                         early[m, at : at + 16] = total[first : first + 16, 128 * t : 128 * t + 128]
-    wide[...] = mm(act[...].T, df[...])
-    for i in range(8):
-        some = wide[pl.ds(pl.multiple_of(64 * xl + 72 * i, 8), 72)]
-        some = jnp.concatenate([some, jnp.zeros((8, 1024), f32)]).astype(low)
-        for r in (0, 1):
-            for t in range(4):
-                early[8 * r + i, 640 + 80 * t : 720 + 80 * t] = some[:, 512 * r + 128 * t : 512 * r + 128 * t + 128]
+            outs[1 + 2 * k + r].start()
+    for copy in outs:
+        copy.wait()
 
 
 def fold(place, keep, got, own, *others):
@@ -584,6 +622,14 @@
             pltpu.VMEM((512, 640), f32),
             pltpu.VMEM((2, 512, 640), low),
             pltpu.VMEM((1024, 512), low),
+            pltpu.VMEM((512, 1024), low),
+            pltpu.VMEM((2, 512, 640), low),
+            pltpu.VMEM((640, 512), low),
+            pltpu.VMEM((512, 1024), f32),
+            pltpu.VMEM((512, 1024), low),
+            pltpu.VMEM((512, 1024), low),
+            pltpu.VMEM((640, 512), low),
+            pltpu.SemaphoreType.DMA((7,)),
         ],
         place,
         *near,
@@ -597,6 +643,8 @@
         *df_near,
         *df_far,
         packs,
+        loose_in=(8, 12, 13),
+        loose_out=(0, 1, 7, 8),
     )
     got = swap_core(send)
     own = shaped(256, 256)
@@ -606,13 +654,22 @@
     (early,) = call(
         feed_weights,
         [shaped(16, 960, 128, kind=low)],
-        [pltpu.VMEM((640, 1024), f32)],
+        [
+            pltpu.VMEM((640, 1024), f32),
+            pltpu.VMEM((16, 960, 128), low),
+            pltpu.VMEM((512, 1024), low),
+            pltpu.VMEM((512, 640), low),
+            pltpu.VMEM((512, 640), low),
+            pltpu.SemaphoreType.DMA((8,)),
+        ],
         place,
         n_two,
         act,
         dgate,
         dup,
         df,
+        loose_in=(0, 2, 3),
+        loose_out=(0,),
     )
     dn_own, early = lax.optimization_barrier((dn_own, early))
     early = early.reshape(16 * 960, 128)

time: 210 us -> 209 us (level)
  no operation moved by 1% of the time
where the time goes in v3:
time: 209 us; the launch traced here: 206 us
  starting transfers between devices  57.2 us (27%)
  Pallas kernels  56.7 us (27%)
  waiting for transfers between devices  50 us (24%)
  local copies, waits for them, and re-layouts  24.1 us (12%)
  between operations  14.9 us (7%)
  other arithmetic  3.02 us (1%)
    pallas_call x13, Pallas kernels, call(): pl.pallas_call(body, out_shape=outs, in_specs=[pl.BlockSpec(memory_space=...  56.7 us
    ppermute x49, waiting for transfers between devices, moved(): return lax.ppermute(value, axes if len(axes) > 1 else axes[0], pairs)  49.9 us
    ppermute x49, starting transfers between devices, moved(): return lax.ppermute(value, axes if len(axes) > 1 else axes[0], pairs)  45.5 us
    all_to_all x1, starting transfers between devices, local(): late = lax.all_to_all(late, ('y', 'z'), 0, 0)  11.6 us
    unnamed x101, local copies, waits for them, and re-layouts  10.2 us
  transfers between devices with their start and end apart: 52, of which 23 were waited for; matrix products, arithmetic and copies ran while one was open for 8% of the time, Pallas kernels for 19%

profile of v3, /device:TPU:38, one launch (start us, length us, event | category | flops | bytes accessed | tf_op | source)
XLA Modules:
  0.0 205.8 jit_solution(18148501733132752934)
XLA Ops:
  12.6 4.3 %collective-permute-done.25 = bf16[128,128]{1,0:T(8,128)(2,1)S(1)} collective-permute-done((bf16[128,128]{1,0:T(8,128)(2,1)S(1)}, bf16[128,128]{1,0:T(8,128)(2,1)S(1)}, u32[]{:S(2)}, u32[]{:S(2)}) %collective-permute-start.25) | collective-permute-done | bytes 32800 | tf_op jit(solution)/shard_map/ppermute | solution.py:35
  26.7 3.3 %constant_dynamic-slice_fusion.8 = bf16[512,2,640]{2,1,0:T(2,128)(2,1)} fusion(bf16[512,2,2304]{2,1,0:T(2,128)(2,1)} %param.17, s32[]{:T(128)S(6)} %select_n.57), kind=kLoop, calls=%fused_computation.19 | loop fusion | bytes 2621444 | tf_op jit(solution)/shard_map/dynamic-slice.1
  35.3 4.1 %collective-permute-done.2.refs_3_ = bf16[1040,256]{1,0:T(8,128)(2,1)S(1)} collective-permute-done((bf16[1040,256]{1,0:T(8,128)(2,1)}, bf16[1040,256]{1,0:T(8,128)(2,1)S(1)}, u32[]{:S(2)}, u32[]{:S(2)}) %collective-permute-start.2) | collective-permute-done | bytes 532512 | tf_op jit(solution)/shard_map/ppermute | solution.py:35
  41.5 4.7 %shard_map.169 = (bf16[512,1024]{1,0:T(8,128)(2,1)}, bf16[512,1024]{1,0:T(8,128)(2,1)}, f32[16,1024]{1,0:T(8,128)}, f32[512,128]{1,0:T(8,128)}, f32[512,128]{1,0...) custom-call(s32[5]{0:T(128)} %stack.55.place, ...), custom_call_target="tpu_custom_call" | custom-call | tf_op jit(solution)/shard_map/pallas_call | solution.py:77
  63.7 3.4 %collective-permute-done.10.refs_2_ = bf16[512,128]{1,0:T(8,128)(2,1)S(1)} collective-permute-done((bf16[512,128]{1,0:T(8,128)(2,1)}, bf16[512,128]{1,0:T(8,128)(2,1)S(1)}, u32[]{:S(2)}, u32[]{:S(2)}) %collective-permute-start.10) | collective-permute-done | bytes 131104 | tf_op jit(solution)/shard_map/ppermute | solution.py:35
  69.2 14.2 %shard_map.171 = (f32[512,1024]{1,0:T(8,128)}, bf16[512,1024]{1,0:T(8,128)(2,1)}, bf16[512,640]{1,0:T(8,128)(2,1)}, bf16[512,640]{1,0:T(8,128)(2,1)}, bf16[512,6...) custom-call(s32[5]{0:T(128)} %stack.55.place, ...), custom_call_target="tpu_custom_call" | custom-call | tf_op jit(solution)/shard_map/pallas_call | solution.py:77
  83.7 5.8 %shard_map.173 = bf16[16,960,128]{2,1,0:T(8,128)(2,1)} custom-call(s32[5]{0:T(128)} %stack.55.place, bf16[512,1024]{1,0:T(8,128)(2,1)} %get-tuple-element.113.n_in, bf16[512,640]{1,0:T(8,128)(2,1)} %get-tuple-element.128.act, bf16[512,640]{1,0:T(8,128)(2,1)} %get-tuple-element.115.dgate_in, bf16[512,640]{1,0:T(8,128)(2,1)} %get-tuple-element.116.dup_in, ...), custom_call_target="tpu_custom_call" | custom-call | tf_op jit(solution)/shard_map/pallas_call | solution.py:77
  94.1 2.8 %collective-permute-start.28 = (bf16[256,256]{1,0:T(8,128)(2,1)S(1)}, bf16[256,256]{1,0:T(8,128)(2,1)S(1)}, u32[]{:S(2)}, u32[]{:S(2)}) collective-permute-start(bf16[256,256]{1,0:T(8,128)(2,1)S(1)} %copy-done.47), channel_id=1, source_target_pairs={{0,2},{2,0},{16,18},{18,16},{1,3},{3,1},{17,19},{19,17},{4,6},{6,4... | collective-permute-start | bytes 393224 | tf_op jit(solution)/shard_map/ppermute | solution.py:35
  99.8 3.7 %collective-permute-done.28 = bf16[256,256]{1,0:T(8,128)(2,1)S(1)} collective-permute-done((bf16[256,256]{1,0:T(8,128)(2,1)S(1)}, bf16[256,256]{1,0:T(8,128)(2,1)S(1)}, u32[]{:S(2)}, u32[]{:S(2)}) %collective-permute-start.28) | collective-permute-done | bytes 131104 | tf_op jit(solution)/shard_map/ppermute | solution.py:35
  107.3 2.8 %collective-permute-start.30 = (bf16[256,256]{1,0:T(8,128)(2,1)S(1)}, bf16[256,256]{1,0:T(8,128)(2,1)S(1)}, u32[]{:S(2)}, u32[]{:S(2)}) collective-permute-start(bf16[256,256]{1,0:T(8,128)(2,1)S(1)} %add_convert_fusion.refs_0_), channel_id=1, source_target_pairs={{0,16},{2,18},{16,0},{18,2},{1,17},{3,19},{17,1},{19,3},{4,20},{6,... | collective-permute-start | bytes 393224 | tf_op jit(solution)/shard_map/ppermute | solution.py:35
  110.1 4.9 %collective-permute-done.32.refs_3_ = bf16[256,256]{1,0:T(8,128)(2,1)S(1)} collective-permute-done((bf16[256,256]{1,0:T(8,128)(2,1)S(1)}, bf16[256,256]{1,0:T(8,128)(2,1)S(1)}, u32[]{:S(2)}, u32[]{:S(2)}) %collective-permute-start.32) | collective-permute-done | bytes 131104 | tf_op jit(solution)/shard_map/ppermute | solution.py:35
  117.7 5.7 %shard_map.174 = (f32[256,256]{1,0:T(8,128)}, bf16[512,1024]{1,0:T(8,128)(2,1)}, f32[512,128]{1,0:T(8,128)}, f32[512,128]{1,0:T(8,128)}, f32[2,16,128]{2,1,0:T(8...) custom-call(s32[5]{0:T(128)} %stack.55.place, bf16[256,256]{1,0:T(8,128)(2,1)} %copy-done.7, bf16[256,256]{1,0:T(8,128)(2,1)} %copy-done.30, ...), custom_call_target="tpu_custom_call" | custom-call | tf_op jit(solution)/shard_map/pallas_call | solution.py:77
  125.4 3.7 %shard_map.175 = (f32[4,256,256]{2,1,0:T(8,128)}, bf16[4,256,256]{2,1,0:T(8,128)(2,1)}) custom-call(s32[5]{0:T(128)} %stack.55.place, bf16[512,640]{1,0:T(8,128)(2,1)} %get-tuple-element.128.act, bf16[640,512]{1,0:T(8,128)(2,1)} %constant_dynamic-slice_fusion.7.refs_13_.down_own, bf16[640,512]{1,0:T(8,128)(2,1)} %get-tuple-element.129.down_far), custom_call_target="tpu_custom_call" | custom-call | tf_op jit(solution)/shard_map/pallas_call | solution.py:77
  129.8 4.3 %shard_map.176 = (bf16[512,384]{1,0:T(8,128)(2,1)}, f32[4,256,256]{2,1,0:T(8,128)}, bf16[4,272,256]{2,1,0:T(8,128)(2,1)}, f32[2,8,256]{2,1,0:T(8,128)}, bf16[2,16,128]{2,1,0:T(8,128)(2,1)}) custom-call(s32[5]{0:T(128)} %stack.55.place, f32[512,128]{1,0:T(8,128)} %get-tuple-element.131.refs_0_, f32[512,128]{1,0:T(8,128)} %get-tuple-element.132.refs_1_, ...), custom_call_target="tpu_custom_call" | custom-call | tf_op jit(solution)/shard_map/pallas_call | solution.py:77
  134.2 3.7 %shard_map.177 = bf16[16,288,128]{2,1,0:T(8,128)(2,1)} custom-call(s32[5]{0:T(128)} %stack.55.place, bf16[512,1024]{1,0:T(8,128)(2,1)} %get-tuple-element.94.n, bf16[512,384]{1,0:T(8,128)(2,1)} %get-tuple-element.141.dproj, bf16[512,128]{1,0:T(8,128)(2,1)} %get-tuple-element.103.refs_0_.y, bf16[512,1024]{1,0:T(8,128)(2,1)} %get-tuple-element.142.do, ...), custom_call_target="tpu_custom_call" | custom-call | tf_op jit(solution)/shard_map/pallas_call | solution.py:77
  137.8 11.6 %all-to-all-start = ((bf16[16,288,128]{2,1,0:T(8,128)(2,1)}), bf16[16,288,128]{2,1,0:T(8,128)(2,1)S(1)}, u32[]{:S(2)}, u32[]{:S(2)}) async-start(bf16[16,288,128]{2,1,0:T(8,128)(2,1)} %shard_map.177), calls=%async_computation | async-start | bytes 2359296 | tf_op jit(solution)/shard_map/all_to_all | solution.py:744
  153.3 3.0 %shard_map.178 = (f32[256,256]{1,0:T(8,128)}, f32[256,256]{1,0:T(8,128)}, f32[8,256]{1,0:T(8,128)}, bf16[528,256]{1,0:T(8,128)(2,1)}, bf16[528,256]{1,0:T(8,128)(2,1)}, /*index=5*/bf16[528,256]{1,0:T(8,128)(2,1)}) custom-call(s32[5]{0:T(128)} %stack.55.place, f32[4,256,256]{2,1,0:T(8,128)} %get-tuple-element.144.keep, bf16[4,272,256]{2,1,0:T(8,128)(2,1)} %copy-done.5, ...), custom_call_target="tpu_custom_call" | custom-call | tf_op jit(solution)/shard_map/pallas_call | solution.py:77
  156.3 2.7 %collective-permute-start.42 = (bf16[528,256]{1,0:T(8,128)(2,1)}, bf16[528,256]{1,0:T(8,128)(2,1)}, u32[]{:S(2)}, u32[]{:S(2)}) collective-permute-start(bf16[528,256]{1,0:T(8,128)(2,1)} %get-tuple-element.153), channel_id=1, source_target_pairs={{0,2},{2,0},{16,18},{18,16},{1,3},{3,1},{17,19},{19,17},{4,6},{6,4... | collective-permute-start | bytes 811016 | tf_op jit(solution)/shard_map/ppermute | solution.py:35
  163.1 2.9 %collective-permute-done.41.got1 = bf16[528,256]{1,0:T(8,128)(2,1)} collective-permute-done((bf16[528,256]{1,0:T(8,128)(2,1)}, bf16[528,256]{1,0:T(8,128)(2,1)}, u32[]{:S(2)}, u32[]{:S(2)}) %collective-permute-start.41) | collective-permute-done | bytes 270368 | tf_op jit(solution)/shard_map/ppermute | solution.py:35
  166.0 5.8 %collective-permute-done.42.got2 = bf16[528,256]{1,0:T(8,128)(2,1)} collective-permute-done((bf16[528,256]{1,0:T(8,128)(2,1)}, bf16[528,256]{1,0:T(8,128)(2,1)}, u32[]{:S(2)}, u32[]{:S(2)}) %collective-permute-start.42) | collective-permute-done | bytes 270368 | tf_op jit(solution)/shard_map/ppermute | solution.py:35
  174.3 2.9 %shard_map.179 = (bf16[256,256]{1,0:T(8,128)(2,1)}, bf16[256,256]{1,0:T(8,128)(2,1)}) custom-call(s32[5]{0:T(128)} %stack.55.place, f32[256,256]{1,0:T(8,128)} %get-tuple-element.149.own, f32[256,256]{1,0:T(8,128)} %get-tuple-element.150.own_ffn, f32[8,256]{1,0:T(8,128)} %get-tuple-element.151.mass, bf16[528,256]{1,0:T(8,128)(2,1)} %collective-permute-done.41.got1, ...), custom_call_target="tpu_custom_call" | custom-call | tf_op jit(solution)/shard_map/pallas_call | solution.py:77
  180.4 3.4 %collective-permute-start.45 = (bf16[224,128]{1,0:T(8,128)(2,1)}, bf16[224,128]{1,0:T(8,128)(2,1)S(1)}, u32[]{:S(2)}, u32[]{:S(2)}) collective-permute-start(bf16[224,128]{1,0:T(8,128)(2,1)} %get-tuple-element.164), channel_id=1, source_target_pairs={{0,2},{2,0},{16,18},{18,16},{1,3},{3,1},{17,19},{19,17},{4,6},{6,4... | collective-permute-start | bytes 172040 | tf_op jit(solution)/shard_map/ppermute | solution.py:35
  185.1 5.9 %collective-permute-start.47 = (bf16[384,128]{1,0:T(8,128)(2,1)}, bf16[384,128]{1,0:T(8,128)(2,1)S(1)}, u32[]{:S(2)}, u32[]{:S(2)}) collective-permute-start(bf16[384,128]{1,0:T(8,128)(2,1)} %get-tuple-element.166), channel_id=1, source_target_pairs={{0,0},{2,64},{4,4},{6,68},{8,8},{10,72},{12,12},{14,76},{16,32},{1... | collective-permute-start | bytes 294920 | tf_op jit(solution)/shard_map/ppermute | solution.py:35
  191.8 3.3 %collective-permute-done.47.settled = bf16[384,128]{1,0:T(8,128)(2,1)S(1)} collective-permute-done((bf16[384,128]{1,0:T(8,128)(2,1)}, bf16[384,128]{1,0:T(8,128)(2,1)S(1)}, u32[]{:S(2)}, u32[]{:S(2)}) %collective-permute-start.47) | collective-permute-done | bytes 98336 | tf_op jit(solution)/shard_map/ppermute | solution.py:35
  (248 shorter events, 77.9 us)
Async XLA Ops:
  7.2 61.9 %all-gather.3.cloned.1.call-start = ((), (), s32[]{:S(2)}) async-start(), calls=%async_computation.3 | async-start | bytes 3342336 | tf_op jit(solution)/shard_map/all_gather | solution.py:554
  18.5 158.8 %reduce-scatter.2.cloned.1.call-start = ((), (), s32[]{:S(2)}) async-start(), calls=%async_computation.2 | async-start | bytes 4177920 | tf_op jit(solution)/shard_map/reduce_scatter | solution.py:676
  18.8 20.7 %collective-permute-start.3 = (bf16[272,256]{1,0:T(8,128)(2,1)S(1)}, bf16[272,256]{1,0:T(8,128)(2,1)}, u32[]{:S(2)}, u32[]{:S(2)}) collective-permute-start(bf16[272,256]{1,0:T(8,128)(2,1)S(1)} %pad_maximum_fusion.4.refs_0_), channel_id=1, source_target_pairs={{0,1},{1,0},{2,3},{3,2},{4,5},{5,4},{6,7},{7,6},{8,9},{9,8},{10,11... | collective-permute-start | bytes 417800 | tf_op jit(solution)/shard_map/ppermute | solution.py:35
  19.0 16.0 %collective-permute-start.1 = (bf16[272,256]{1,0:T(8,128)(2,1)S(1)}, bf16[272,256]{1,0:T(8,128)(2,1)}, u32[]{:S(2)}, u32[]{:S(2)}) collective-permute-start(bf16[272,256]{1,0:T(8,128)(2,1)S(1)} %pad_maximum_fusion.4.refs_0_), channel_id=1, source_target_pairs={{0,2},{2,0},{16,18},{18,16},{1,3},{3,1},{17,19},{19,17},{4,6},{6,4... | collective-permute-start | bytes 417800 | tf_op jit(solution)/shard_map/ppermute | solution.py:35
  19.2 15.6 %collective-permute-start = (bf16[272,256]{1,0:T(8,128)(2,1)S(1)}, bf16[272,256]{1,0:T(8,128)(2,1)}, u32[]{:S(2)}, u32[]{:S(2)}) collective-permute-start(bf16[272,256]{1,0:T(8,128)(2,1)S(1)} %pad_maximum_fusion.4.refs_0_), channel_id=1, source_target_pairs={{0,16},{2,18},{16,0},{18,2},{1,17},{3,19},{17,1},{19,3},{4,20},{6,... | collective-permute-start | bytes 417800 | tf_op jit(solution)/shard_map/ppermute | solution.py:35
  20.5 34.8 %collective-permute-start.16 = (bf16[512,512]{1,0:T(8,128)(2,1)S(1)}, bf16[512,512]{1,0:T(8,128)(2,1)}, u32[]{:S(2)}, u32[]{:S(2)}) collective-permute-start(bf16[512,512]{1,0:T(8,128)(2,1)S(1)} %copy-done.3), channel_id=1, source_target_pairs={{0,1},{1,0},{2,3},{3,2},{4,5},{5,4},{6,7},{7,6},{8,9},{9,8},{10,11... | collective-permute-start | bytes 1572872 | tf_op jit(solution)/shard_map/ppermute | solution.py:35
  23.4 15.9 %collective-permute-start.2 = (bf16[1040,256]{1,0:T(8,128)(2,1)}, bf16[1040,256]{1,0:T(8,128)(2,1)S(1)}, u32[]{:S(2)}, u32[]{:S(2)}) collective-permute-start(bf16[1040,256]{1,0:T(8,128)(2,1)} %pad_maximum_fusion), channel_id=1, source_target_pairs={{0,18},{2,16},{16,2},{18,0},{1,19},{3,17},{17,3},{19,1},{4,22},{6,... | collective-permute-start | bytes 1597448 | tf_op jit(solution)/shard_map/ppermute | solution.py:35
  48.8 9.2 %collective-permute-start.20 = (bf16[256,256]{1,0:T(8,128)(2,1)S(1)}, bf16[256,256]{1,0:T(8,128)(2,1)S(1)}, u32[]{:S(2)}, u32[]{:S(2)}) collective-permute-start(bf16[256,256]{1,0:T(8,128)(2,1)S(1)} %copy-done.14), channel_id=1, source_target_pairs={{0,1},{1,0},{2,3},{3,2},{4,5},{5,4},{6,7},{7,6},{8,9},{9,8},{10,11... | collective-permute-start | bytes 393224 | tf_op jit(solution)/shard_map/ppermute | solution.py:35
  48.9 9.3 %collective-permute-start.19 = (bf16[256,256]{1,0:T(8,128)(2,1)S(1)}, bf16[256,256]{1,0:T(8,128)(2,1)S(1)}, u32[]{:S(2)}, u32[]{:S(2)}) collective-permute-start(bf16[256,256]{1,0:T(8,128)(2,1)S(1)} %copy-done.14), channel_id=1, source_target_pairs={{0,18},{2,16},{16,2},{18,0},{1,19},{3,17},{17,3},{19,1},{4,22},{6,... | collective-permute-start | bytes 393224 | tf_op jit(solution)/shard_map/ppermute | solution.py:35
  51.6 7.9 %collective-permute-start.18 = (bf16[256,256]{1,0:T(8,128)(2,1)S(1)}, bf16[256,256]{1,0:T(8,128)(2,1)S(1)}, u32[]{:S(2)}, u32[]{:S(2)}) collective-permute-start(bf16[256,256]{1,0:T(8,128)(2,1)S(1)} %copy-done.14), channel_id=1, source_target_pairs={{0,2},{2,0},{16,18},{18,16},{1,3},{3,1},{17,19},{19,17},{4,6},{6,4... | collective-permute-start | bytes 393224 | tf_op jit(solution)/shard_map/ppermute | solution.py:35
  51.6 8.7 %collective-permute-start.17 = (bf16[256,256]{1,0:T(8,128)(2,1)S(1)}, bf16[256,256]{1,0:T(8,128)(2,1)S(1)}, u32[]{:S(2)}, u32[]{:S(2)}) collective-permute-start(bf16[256,256]{1,0:T(8,128)(2,1)S(1)} %copy-done.14), channel_id=1, source_target_pairs={{0,16},{2,18},{16,0},{18,2},{1,17},{3,19},{17,1},{19,3},{4,20},{6,... | collective-permute-start | bytes 393224 | tf_op jit(solution)/shard_map/ppermute | solution.py:35
  59.5 7.6 %collective-permute-start.10 = (bf16[512,128]{1,0:T(8,128)(2,1)}, bf16[512,128]{1,0:T(8,128)(2,1)S(1)}, u32[]{:S(2)}, u32[]{:S(2)}) collective-permute-start(bf16[512,128]{1,0:T(8,128)(2,1)} %get-tuple-element.103.refs_0_.y), channel_id=1, source_target_pairs={{0,2},{2,0},{16,18},{18,16},{1,3},{3,1},{17,19},{19,17},{4,6},{6,4... | collective-permute-start | bytes 393224 | tf_op jit(solution)/shard_map/ppermute | solution.py:35
  94.1 9.4 %collective-permute-start.28 = (bf16[256,256]{1,0:T(8,128)(2,1)S(1)}, bf16[256,256]{1,0:T(8,128)(2,1)S(1)}, u32[]{:S(2)}, u32[]{:S(2)}) collective-permute-start(bf16[256,256]{1,0:T(8,128)(2,1)S(1)} %copy-done.47), channel_id=1, source_target_pairs={{0,2},{2,0},{16,18},{18,16},{1,3},{3,1},{17,19},{19,17},{4,6},{6,4... | collective-permute-start | bytes 393224 | tf_op jit(solution)/shard_map/ppermute | solution.py:35
  96.9 8.9 %collective-permute-start.29 = (bf16[256,256]{1,0:T(8,128)(2,1)S(1)}, bf16[256,256]{1,0:T(8,128)(2,1)S(1)}, u32[]{:S(2)}, u32[]{:S(2)}) collective-permute-start(bf16[256,256]{1,0:T(8,128)(2,1)S(1)} %copy-done.46), channel_id=1, source_target_pairs={{0,18},{2,16},{16,2},{18,0},{1,19},{3,17},{17,3},{19,1},{4,22},{6,... | collective-permute-start | bytes 393224 | tf_op jit(solution)/shard_map/ppermute | solution.py:35
  105.9 9.1 %collective-permute-start.32 = (bf16[256,256]{1,0:T(8,128)(2,1)S(1)}, bf16[256,256]{1,0:T(8,128)(2,1)S(1)}, u32[]{:S(2)}, u32[]{:S(2)}) collective-permute-start(bf16[256,256]{1,0:T(8,128)(2,1)S(1)} %add_convert_fusion.refs_0_), channel_id=1, source_target_pairs={{0,18},{2,16},{16,2},{18,0},{1,19},{3,17},{17,3},{19,1},{4,22},{6,... | collective-permute-start | bytes 393224 | tf_op jit(solution)/shard_map/ppermute | solution.py:35
  107.3 7.8 %collective-permute-start.31 = (bf16[256,256]{1,0:T(8,128)(2,1)S(1)}, bf16[256,256]{1,0:T(8,128)(2,1)S(1)}, u32[]{:S(2)}, u32[]{:S(2)}) collective-permute-start(bf16[256,256]{1,0:T(8,128)(2,1)S(1)} %add_convert_fusion.refs_0_), channel_id=1, source_target_pairs={{0,2},{2,0},{16,18},{18,16},{1,3},{3,1},{17,19},{19,17},{4,6},{6,4... | collective-permute-start | bytes 393224 | tf_op jit(solution)/shard_map/ppermute | solution.py:35
  107.3 8.4 %collective-permute-start.30 = (bf16[256,256]{1,0:T(8,128)(2,1)S(1)}, bf16[256,256]{1,0:T(8,128)(2,1)S(1)}, u32[]{:S(2)}, u32[]{:S(2)}) collective-permute-start(bf16[256,256]{1,0:T(8,128)(2,1)S(1)} %add_convert_fusion.refs_0_), channel_id=1, source_target_pairs={{0,16},{2,18},{16,0},{18,2},{1,17},{3,19},{17,1},{19,3},{4,20},{6,... | collective-permute-start | bytes 393224 | tf_op jit(solution)/shard_map/ppermute | solution.py:35
  137.8 39.4 %all-to-all-start = ((bf16[16,288,128]{2,1,0:T(8,128)(2,1)}), bf16[16,288,128]{2,1,0:T(8,128)(2,1)S(1)}, u32[]{:S(2)}, u32[]{:S(2)}) async-start(bf16[16,288,128]{2,1,0:T(8,128)(2,1)} %shard_map.177), calls=%async_computation | async-start | bytes 2359296 | tf_op jit(solution)/shard_map/all_to_all | solution.py:744
  156.3 9.6 %collective-permute-start.41 = (bf16[528,256]{1,0:T(8,128)(2,1)}, bf16[528,256]{1,0:T(8,128)(2,1)}, u32[]{:S(2)}, u32[]{:S(2)}) collective-permute-start(bf16[528,256]{1,0:T(8,128)(2,1)} %get-tuple-element.152), channel_id=1, source_target_pairs={{0,16},{2,18},{16,0},{18,2},{1,17},{3,19},{17,1},{19,3},{4,20},{6,... | collective-permute-start | bytes 811016 | tf_op jit(solution)/shard_map/ppermute | solution.py:35
  156.3 15.4 %collective-permute-start.42 = (bf16[528,256]{1,0:T(8,128)(2,1)}, bf16[528,256]{1,0:T(8,128)(2,1)}, u32[]{:S(2)}, u32[]{:S(2)}) collective-permute-start(bf16[528,256]{1,0:T(8,128)(2,1)} %get-tuple-element.153), channel_id=1, source_target_pairs={{0,2},{2,0},{16,18},{18,16},{1,3},{3,1},{17,19},{19,17},{4,6},{6,4... | collective-permute-start | bytes 811016 | tf_op jit(solution)/shard_map/ppermute | solution.py:35
  159.1 15.3 %collective-permute-start.43 = (bf16[528,256]{1,0:T(8,128)(2,1)}, bf16[528,256]{1,0:T(8,128)(2,1)}, u32[]{:S(2)}, u32[]{:S(2)}) collective-permute-start(bf16[528,256]{1,0:T(8,128)(2,1)} %get-tuple-element.154), channel_id=1, source_target_pairs={{0,18},{2,16},{16,2},{18,0},{1,19},{3,17},{17,3},{19,1},{4,22},{6,... | collective-permute-start | bytes 811016 | tf_op jit(solution)/shard_map/ppermute | solution.py:35
  180.4 10.6 %collective-permute-start.44 = (bf16[224,128]{1,0:T(8,128)(2,1)}, bf16[224,128]{1,0:T(8,128)(2,1)S(1)}, u32[]{:S(2)}, u32[]{:S(2)}) collective-permute-start(bf16[224,128]{1,0:T(8,128)(2,1)} %get-tuple-element.163), channel_id=1, source_target_pairs={{0,16},{2,18},{16,0},{18,2},{1,17},{3,19},{17,1},{19,3},{4,20},{6,... | collective-permute-start | bytes 172040 | tf_op jit(solution)/shard_map/ppermute | solution.py:35
  180.4 10.6 %collective-permute-start.45 = (bf16[224,128]{1,0:T(8,128)(2,1)}, bf16[224,128]{1,0:T(8,128)(2,1)S(1)}, u32[]{:S(2)}, u32[]{:S(2)}) collective-permute-start(bf16[224,128]{1,0:T(8,128)(2,1)} %get-tuple-element.164), channel_id=1, source_target_pairs={{0,2},{2,0},{16,18},{18,16},{1,3},{3,1},{17,19},{19,17},{4,6},{6,4... | collective-permute-start | bytes 172040 | tf_op jit(solution)/shard_map/ppermute | solution.py:35
  185.1 10.0 %collective-permute-start.47 = (bf16[384,128]{1,0:T(8,128)(2,1)}, bf16[384,128]{1,0:T(8,128)(2,1)S(1)}, u32[]{:S(2)}, u32[]{:S(2)}) collective-permute-start(bf16[384,128]{1,0:T(8,128)(2,1)} %get-tuple-element.166), channel_id=1, source_target_pairs={{0,0},{2,64},{4,4},{6,68},{8,8},{10,72},{12,12},{14,76},{16,32},{1... | collective-permute-start | bytes 294920 | tf_op jit(solution)/shard_map/ppermute | solution.py:35
  (79 other events, 346.0 us)
Sparse Core Ops, SparseCore 0:
  18.6 49.0 all-gather.2
  92.8 82.6 reduce-scatter.1
